TPU v7x, 128 devices: a whole 4x4x4 slice. The times are simulated.
128 devices in a mesh: seq: 32 (over z, y, core), head: 4 (over x).
Axes of the slice: x: 4, y: 4, z: 4, core: 2. Of those that a mesh axis runs over, the one named last changes fastest.
Arguments:
- query: bfloat16 [65536, 1024], P('seq', 'head'), may hold values from -6 to 6
- keys: bfloat16 [65536, 1024], P('seq', 'head'), may hold values from -6 to 6
- values: bfloat16 [65536, 1024], P('seq', 'head'), may hold values from -6 to 6
- output: bfloat16 [65536, 1024], P('seq', 'head'), may hold values from -6 to 6
- d_out: bfloat16 [65536, 1024], P(('seq', 'head')), may hold values from -1.5 to 1.5
- row_logsum: float32 [8, 65536], P('head', 'seq'), may hold values from 3.5 to 4.5
- selected: int32 [128, 3], replicated, may hold values from 0 to 123, as said below
Outputs:
- query_grad: bfloat16 [65536, 1024], P('seq', 'head')
- key_grad: bfloat16 [65536, 1024], P('seq', 'head')
- value_grad: bfloat16 [65536, 1024], P('seq', 'head')
Inputs may be any that keep to these rules, and one draw needn't show every extreme that they name: `selected`: each nonzero entry of row g names a block other than block 0 that is held by a seq index lower than the seq index holding block g. Among the 12 entries of the query blocks of one seq index, at most one names a block of any one other seq index.
All inputs are finite; a program needn't handle non-finite values.
Results may differ from a plain program's by a relative error of at most 0.0063.
Values may be sent and summed in bfloat16 or wider, within the bound.
A program may use at most 192 MiB of HBM per device.

v0:
```python
import math

import jax
import jax.numpy as jnp
from jax import lax
from jax.sharding import PartitionSpec as P

BLOCK = 512


def from_root(value, axis, source):
    kept = jnp.where(lax.axis_index(axis) == source, value, 0).astype(value.dtype)
    return lax.psum(kept, axis)


def block_terms(query_blk, grad_blk, logsum_blk, delta_blk, key_stack, value_stack, mask, scale):
    heads = logsum_blk.shape[0]
    length = query_blk.shape[0]
    width = query_blk.shape[1]
    head_dim = width // heads
    stacked = key_stack.shape[0]
    query_heads = query_blk.reshape(length, heads, head_dim)
    grad_heads = grad_blk.reshape(length, heads, head_dim)
    key_heads = key_stack.reshape(stacked, length, heads, head_dim)
    value_heads = value_stack.reshape(stacked, length, heads, head_dim)
    scores = (
        jnp.einsum("ihd,bjhd->hibj", query_heads, key_heads, preferred_element_type=jnp.float32)
        * scale
    )
    weights = jnp.where(mask[None], jnp.exp(scores - logsum_blk[:, :, None, None]), 0.0)
    weight_grad = jnp.einsum(
        "ihd,bjhd->hibj", grad_heads, value_heads, preferred_element_type=jnp.float32
    )
    score_grad = (weights * (weight_grad - delta_blk[:, :, None, None])).astype(jnp.bfloat16)
    weights_low = weights.astype(jnp.bfloat16)
    query_grad = (
        jnp.einsum("hibj,bjhd->ihd", score_grad, key_heads, preferred_element_type=jnp.float32)
        * scale
    )
    key_term = (
        jnp.einsum("hibj,ihd->bjhd", score_grad, query_heads, preferred_element_type=jnp.float32)
        * scale
    )
    value_term = jnp.einsum(
        "hibj,ihd->bjhd", weights_low, grad_heads, preferred_element_type=jnp.float32
    )
    return (
        query_grad.reshape(length, width),
        key_term.reshape(stacked, length, width),
        value_term.reshape(stacked, length, width),
    )


def body(query, keys, values, output, d_out, row_logsum, selected):
    seq_count = lax.axis_size("seq")
    position = lax.axis_index("seq")
    heads = row_logsum.shape[0]
    tokens = query.shape[0]
    width = query.shape[1]
    head_dim = width // heads
    blocks = tokens // BLOCK
    picks = selected.shape[1]
    scale = 1.0 / math.sqrt(head_dim)
    grad_out = lax.all_to_all(d_out, "head", split_axis=1, concat_axis=0, tiled=True)
    delta = jnp.sum(
        (grad_out.astype(jnp.float32) * output.astype(jnp.float32)).reshape(
            tokens, heads, head_dim
        ),
        axis=2,
    )
    delta = jnp.transpose(delta.reshape(blocks, BLOCK, heads), (0, 2, 1))
    logsum = jnp.transpose(row_logsum.reshape(heads, blocks, BLOCK), (1, 0, 2))
    table = selected.reshape(seq_count, blocks * picks)
    owners = table // blocks
    offsets = table % blocks
    mine = (table > 0) & (owners == position)
    block_ids = jnp.arange(blocks, dtype=jnp.int32)
    peers = jnp.arange(seq_count, dtype=jnp.int32)
    send_map = jnp.sum(
        jnp.where(mine[:, :, None] & (offsets[:, :, None] == block_ids[None, None, :]), 1.0, 0.0),
        axis=1,
    )
    key_blocks = keys.reshape(blocks, BLOCK, width)
    value_blocks = values.reshape(blocks, BLOCK, width)
    query_blocks = query.reshape(blocks, BLOCK, width)
    grad_blocks = grad_out.reshape(blocks, BLOCK, width)
    own_rows = lax.dynamic_slice_in_dim(selected, position * blocks, blocks, 0)
    route_low = send_map.astype(jnp.bfloat16)
    send_keys = jnp.einsum(
        "rb,bte->rte", route_low, key_blocks, preferred_element_type=jnp.float32
    ).astype(jnp.bfloat16)
    send_values = jnp.einsum(
        "rb,bte->rte", route_low, value_blocks, preferred_element_type=jnp.float32
    ).astype(jnp.bfloat16)
    got_keys, got_values = (
        lax.all_to_all(send_keys, "seq", split_axis=0, concat_axis=0, tiled=True),
        lax.all_to_all(send_values, "seq", split_axis=0, concat_axis=0, tiled=True),
    )
    first_key, first_value = (
        from_root(key_blocks[0], "seq", 0),
        from_root(value_blocks[0], "seq", 0),
    )
    positions = jnp.arange(BLOCK, dtype=jnp.int32)
    causal = positions[None, :] <= positions[:, None]
    global_ids = position * blocks + block_ids
    slots = jnp.arange(picks + 2, dtype=jnp.int32)

    def one_block(inputs):
        query_blk, grad_blk, logsum_blk, delta_blk, own_key, own_value, chosen, block_id = inputs
        sources = chosen // blocks
        picked_keys = jnp.take(got_keys, sources, axis=0)
        picked_values = jnp.take(got_values, sources, axis=0)
        key_stack = jnp.concatenate([own_key[None], first_key[None], picked_keys], axis=0)
        value_stack = jnp.concatenate([own_value[None], first_value[None], picked_values], axis=0)
        active = jnp.concatenate(
            [jnp.ones((1,), bool), jnp.reshape(block_id >= 1, (1,)), chosen > 0]
        )
        mask = jnp.where((slots == 0)[None, :, None], causal[:, None, :], active[None, :, None])
        query_part, key_term, value_term = block_terms(
            query_blk, grad_blk, logsum_blk, delta_blk, key_stack, value_stack, mask, scale
        )
        return (
            query_part.astype(jnp.bfloat16),
            key_term[0],
            value_term[0],
            key_term[1],
            value_term[1],
            key_term[2:].astype(jnp.bfloat16),
            value_term[2:].astype(jnp.bfloat16),
        )

    results = lax.map(
        one_block,
        (query_blocks, grad_blocks, logsum, delta, key_blocks, value_blocks, own_rows, global_ids),
    )
    query_grad, own_keys, own_values, first_keys, first_values, picked_keys, picked_values = results
    flat_owner = (own_rows // blocks).reshape(-1)
    flat_live = (own_rows > 0).reshape(-1)
    back_map = jnp.where(
        flat_live[None, :] & (flat_owner[None, :] == peers[:, None]), 1.0, 0.0
    ).astype(jnp.bfloat16)
    back_keys = jnp.einsum(
        "pm,mte->pte",
        back_map,
        picked_keys.reshape(blocks * picks, BLOCK, width),
        preferred_element_type=jnp.float32,
    ).astype(jnp.bfloat16)
    back_values = jnp.einsum(
        "pm,mte->pte",
        back_map,
        picked_values.reshape(blocks * picks, BLOCK, width),
        preferred_element_type=jnp.float32,
    ).astype(jnp.bfloat16)
    returned_keys, returned_values = (
        lax.all_to_all(back_keys, "seq", split_axis=0, concat_axis=0, tiled=True),
        lax.all_to_all(back_values, "seq", split_axis=0, concat_axis=0, tiled=True),
    )
    send_low = send_map.astype(jnp.bfloat16)
    key_total = own_keys + jnp.einsum(
        "rb,rte->bte", send_low, returned_keys, preferred_element_type=jnp.float32
    )
    value_total = own_values + jnp.einsum(
        "rb,rte->bte", send_low, returned_values, preferred_element_type=jnp.float32
    )
    first_key_sum, first_value_sum = lax.psum(
        (jnp.sum(first_keys, axis=0), jnp.sum(first_values, axis=0)), "seq"
    )
    leading = ((block_ids == 0) & (position == 0))[:, None, None]
    key_total = key_total + jnp.where(leading, first_key_sum[None], 0.0)
    value_total = value_total + jnp.where(leading, first_value_sum[None], 0.0)
    return (
        query_grad.reshape(tokens, width),
        key_total.reshape(tokens, width).astype(jnp.bfloat16),
        value_total.reshape(tokens, width).astype(jnp.bfloat16),
    )


def solution(mesh):
    in_specs = (
        P("seq", "head"),
        P("seq", "head"),
        P("seq", "head"),
        P("seq", "head"),
        P(("seq", "head"), None),
        P("head", "seq"),
        P(),
    )
    out_specs = (P("seq", "head"), P("seq", "head"), P("seq", "head"))
    return jax.shard_map(body, mesh=mesh, in_specs=in_specs, out_specs=out_specs, check_vma=False)
```

profile of v0, /device:TPU:0, one launch (start us, length us, event | category | flops | bytes accessed | tf_op | source)
XLA Modules:
  0.0 1005.6 jit_solution(15705548728068079006)
XLA Ops:
  19.2 11.5 %copy.157 = bf16[32,512,256]{2,1,0:T(8,128)(2,1)} copy(bf16[32,512,256]{2,0,1:T(8,128)(2,1)} %convolution_convert_fusion.3) | data formatting | bytes 16777216 | tf_op jit(solution)/shard_map/convert_element_type | solution.py:91
  30.7 8.8 all-to-all-start
  44.3 11.4 %copy.161 = bf16[32,512,256]{2,1,0:T(8,128)(2,1)} copy(bf16[32,512,256]{2,0,1:T(8,128)(2,1)} %convolution_convert_fusion.2) | data formatting | bytes 16777216 | tf_op jit(solution)/shard_map/convert_element_type | solution.py:94
  55.7 89.6 %all-to-all-done = bf16[32,512,256]{2,1,0:T(8,128)(2,1)} async-done(((bf16[32,512,256]{2,1,0:T(8,128)(2,1)}), bf16[32,512,256]{2,1,0:T(8,128)(2,1)}, u32[]{:S(2)}, u32[]{:S(2)}) %all-to-all-start) | async-done | bytes 8388640 | tf_op jit(solution)/shard_map/all_to_all | solution.py:96
  167.9 153.3 %all-reduce.7.cloned.1.call-done = (bf16[512,256]{0,1:T(8,128)(2,1)}, bf16[512,256]{0,1:T(8,128)(2,1)}) async-done(((bf16[512,256]{0,1:T(8,128)(2,1)}, bf16[512,256]{0,1:T(8,128)(2,1)}), (bf16[512,256]{0,1:T(8,128)(2,1)}, bf16[512,256]{0,1:T(8,128)(2,1)})) %all-reduce.7.cloned.1.call-update) | async-done | bytes 524304 | tf_op jit(solution)/shard_map/psum | solution.py:13
  321.2 337.1 %while.26 = (s32[]{:T(128)}, bf16[4,512,256]{2,1,0:T(8,128)(2,1)}, f32[4,512,256]{2,0,1:T(4,128)}, f32[4,512,256]{2,0,1:T(4,128)}, f32[4,512,256]{1,2,0:T(8,128)...) while((s32[]{:T(128)}, bf16[4,512,256]{2,1,0:T(8,128)(2,1)}, ...), condition=%wide.region_5.7_spmd.clone.clone, body=%wide.region_4.6_spmd.clone.sunk.clone | while | flops 3394110464 | bytes 143434272 | solution.py:132
  349.3 6.9 multiply_convert_fusion.3
  365.6 12.2 %dynamic_update_slice.70 = f32[4,512,256]{2,0,1:T(4,128)} dynamic-update-slice(f32[4,512,256]{2,0,1:T(4,128)} %get-tuple-element.724, f32[1,512,256]{2,0,1:T(1,128)} %copy.273, s32[]{:T(128)S(6)} %copy.294, s32[]{:T(128)} %constant.136.clone.1..sunk.1, s32[]{:T(128)} %constant.136.clone.1..sunk.1) | dynamic-update-slice | bytes 1048580 | tf_op jit(solution)/shard_map/while/body/jit(dynamic_update_index_in_dim)/dynamic_update_slice | solution.py:132
  388.3 12.2 %dynamic_update_slice.71 = f32[4,512,256]{2,0,1:T(4,128)} dynamic-update-slice(f32[4,512,256]{2,0,1:T(4,128)} %get-tuple-element.725, f32[1,512,256]{2,0,1:T(1,128)} %copy.274, s32[]{:T(128)S(6)} %copy.294, s32[]{:T(128)} %constant.136.clone.1..sunk.1, s32[]{:T(128)} %constant.136.clone.1..sunk.1) | dynamic-update-slice | bytes 1048580 | tf_op jit(solution)/shard_map/while/body/jit(dynamic_update_index_in_dim)/dynamic_update_slice | solution.py:132
  449.8 12.2 %dynamic_update_slice.70 = f32[4,512,256]{2,0,1:T(4,128)} dynamic-update-slice(f32[4,512,256]{2,0,1:T(4,128)} %get-tuple-element.724, f32[1,512,256]{2,0,1:T(1,128)} %copy.273, s32[]{:T(128)S(6)} %copy.294, s32[]{:T(128)} %constant.136.clone.1..sunk.1, s32[]{:T(128)} %constant.136.clone.1..sunk.1) | dynamic-update-slice | bytes 1048580 | tf_op jit(solution)/shard_map/while/body/jit(dynamic_update_index_in_dim)/dynamic_update_slice | solution.py:132
  472.5 12.2 %dynamic_update_slice.71 = f32[4,512,256]{2,0,1:T(4,128)} dynamic-update-slice(f32[4,512,256]{2,0,1:T(4,128)} %get-tuple-element.725, f32[1,512,256]{2,0,1:T(1,128)} %copy.274, s32[]{:T(128)S(6)} %copy.294, s32[]{:T(128)} %constant.136.clone.1..sunk.1, s32[]{:T(128)} %constant.136.clone.1..sunk.1) | dynamic-update-slice | bytes 1048580 | tf_op jit(solution)/shard_map/while/body/jit(dynamic_update_index_in_dim)/dynamic_update_slice | solution.py:132
  534.0 12.2 %dynamic_update_slice.70 = f32[4,512,256]{2,0,1:T(4,128)} dynamic-update-slice(f32[4,512,256]{2,0,1:T(4,128)} %get-tuple-element.724, f32[1,512,256]{2,0,1:T(1,128)} %copy.273, s32[]{:T(128)S(6)} %copy.294, s32[]{:T(128)} %constant.136.clone.1..sunk.1, s32[]{:T(128)} %constant.136.clone.1..sunk.1) | dynamic-update-slice | bytes 1048580 | tf_op jit(solution)/shard_map/while/body/jit(dynamic_update_index_in_dim)/dynamic_update_slice | solution.py:132
  556.6 12.2 %dynamic_update_slice.71 = f32[4,512,256]{2,0,1:T(4,128)} dynamic-update-slice(f32[4,512,256]{2,0,1:T(4,128)} %get-tuple-element.725, f32[1,512,256]{2,0,1:T(1,128)} %copy.274, s32[]{:T(128)S(6)} %copy.294, s32[]{:T(128)} %constant.136.clone.1..sunk.1, s32[]{:T(128)} %constant.136.clone.1..sunk.1) | dynamic-update-slice | bytes 1048580 | tf_op jit(solution)/shard_map/while/body/jit(dynamic_update_index_in_dim)/dynamic_update_slice | solution.py:132
  618.2 12.2 %dynamic_update_slice.70 = f32[4,512,256]{2,0,1:T(4,128)} dynamic-update-slice(f32[4,512,256]{2,0,1:T(4,128)} %get-tuple-element.724, f32[1,512,256]{2,0,1:T(1,128)} %copy.273, s32[]{:T(128)S(6)} %copy.294, s32[]{:T(128)} %constant.136.clone.1..sunk.1, s32[]{:T(128)} %constant.136.clone.1..sunk.1) | dynamic-update-slice | bytes 1048580 | tf_op jit(solution)/shard_map/while/body/jit(dynamic_update_index_in_dim)/dynamic_update_slice | solution.py:132
  640.8 12.2 %dynamic_update_slice.71 = f32[4,512,256]{2,0,1:T(4,128)} dynamic-update-slice(f32[4,512,256]{2,0,1:T(4,128)} %get-tuple-element.725, f32[1,512,256]{2,0,1:T(1,128)} %copy.274, s32[]{:T(128)S(6)} %copy.294, s32[]{:T(128)} %constant.136.clone.1..sunk.1, s32[]{:T(128)} %constant.136.clone.1..sunk.1) | dynamic-update-slice | bytes 1048580 | tf_op jit(solution)/shard_map/while/body/jit(dynamic_update_index_in_dim)/dynamic_update_slice | solution.py:132
  658.4 8.0 copy.173
  666.3 7.9 convolution_convert_fusion.1
  674.2 11.4 %copy.174 = bf16[32,512,256]{2,1,0:T(8,128)(2,1)} copy(bf16[32,512,256]{2,0,1:T(8,128)(2,1)} %convolution_convert_fusion.1) | data formatting | bytes 16777216 | tf_op jit(solution)/shard_map/convert_element_type | solution.py:147
  697.4 7.9 convolution_convert_fusion
  705.2 11.4 %copy.180 = bf16[32,512,256]{2,1,0:T(8,128)(2,1)} copy(bf16[32,512,256]{2,0,1:T(8,128)(2,1)} %convolution_convert_fusion) | data formatting | bytes 16777216 | tf_op jit(solution)/shard_map/convert_element_type | solution.py:153
  716.6 80.9 %all-to-all-done.3 = bf16[32,512,256]{2,1,0:T(8,128)(2,1)} async-done(((bf16[32,512,256]{2,1,0:T(8,128)(2,1)}), bf16[32,512,256]{2,1,0:T(8,128)(2,1)}, u32[]{:S(2)}, u32[]{:S(2)}) %all-to-all-start.3) | async-done | bytes 8388640 | tf_op jit(solution)/shard_map/all_to_all | solution.py:155
  806.7 169.2 %all-reduce.5.cloned.1.call-done = (f32[512,256]{0,1:T(8,128)}, f32[512,256]{0,1:T(8,128)}) async-done(((f32[512,256]{0,1:T(8,128)}, f32[512,256]{0,1:T(8,128)}), (f32[512,256]{0,1:T(8,128)}, f32[512,256]{0,1:T(8,128)})) %all-reduce.5.cloned.1.call-update) | async-done | bytes 1048592 | tf_op jit(solution)/shard_map/psum | solution.py:165
  978.4 8.6 add_convert_fusion.1
  988.1 9.1 add_convert_fusion
  (299 shorter events, 293.2 us)
Async XLA Ops:
  7.2 6.8 copy-start.14
  7.2 7.2 copy-start.4
  9.6 21.1 %all-to-all-start.1 = ((bf16[512,4,256]{0,2,1:T(8,128)(2,1)}), bf16[512,4,256]{0,2,1:T(8,128)(2,1)S(1)}, u32[]{:S(2)}, u32[]{:S(2)}) async-start(bf16[512,4,256]{0,2,1:T(8,128)(2,1)} %bitcast.5), calls=%async_computation.1 | async-start | bytes 2097152 | tf_op jit(solution)/shard_map/all_to_all | solution.py:64
  14.4 25.1 %copy-start.10 = (bf16[32,4]{0,1:T(4,128)(2,1)}, bf16[32,4]{0,1:T(4,128)(2,1)S(1)}, u32[]{:S(2)}) copy-start(bf16[32,4]{0,1:T(4,128)(2,1)S(1)} %select_reduce_fusion) | copy-start | bytes 772
  30.7 8.8 copy-start.5
  30.7 114.6 %all-to-all-start = ((bf16[32,512,256]{2,1,0:T(8,128)(2,1)}), bf16[32,512,256]{2,1,0:T(8,128)(2,1)}, u32[]{:S(2)}, u32[]{:S(2)}) async-start(bf16[32,512,256]{2,1,0:T(8,128)(2,1)} %copy.157), calls=%async_computation | async-start | bytes 16777216 | tf_op jit(solution)/shard_map/all_to_all | solution.py:96
  145.3 175.9 %all-to-all-start.2 = ((bf16[32,512,256]{2,1,0:T(8,128)(2,1)}), bf16[32,512,256]{2,1,0:T(8,128)(2,1)}, u32[]{:S(2)}, u32[]{:S(2)}) async-start(bf16[32,512,256]{2,1,0:T(8,128)(2,1)} %copy.161), calls=%async_computation.2 | async-start | bytes 16777216 | tf_op jit(solution)/shard_map/all_to_all | solution.py:97
  150.3 170.9 %all-reduce.7.cloned.1.call-start = ((), (), s32[]{:S(2)}) async-start(), calls=%async_computation.6 | async-start | bytes 1048576 | tf_op jit(solution)/shard_map/psum | solution.py:13
  345.4 3.9 copy-start.6
  362.8 15.0 %copy-start.7 = (bf16[1,512,256]{1,2,0:T(8,128)(2,1)S(1)}, bf16[1,512,256]{1,2,0:T(8,128)(2,1)}, u32[]{:S(2)}) copy-start(bf16[1,512,256]{1,2,0:T(8,128)(2,1)} %copy-done.6) | copy-start | bytes 786436 | tf_op jit(solution)/shard_map/while
  447.0 15.0 %copy-start.7 = (bf16[1,512,256]{1,2,0:T(8,128)(2,1)S(1)}, bf16[1,512,256]{1,2,0:T(8,128)(2,1)}, u32[]{:S(2)}) copy-start(bf16[1,512,256]{1,2,0:T(8,128)(2,1)} %copy-done.6) | copy-start | bytes 786436 | tf_op jit(solution)/shard_map/while
  513.7 3.9 copy-start.6
  531.1 15.0 %copy-start.7 = (bf16[1,512,256]{1,2,0:T(8,128)(2,1)S(1)}, bf16[1,512,256]{1,2,0:T(8,128)(2,1)}, u32[]{:S(2)}) copy-start(bf16[1,512,256]{1,2,0:T(8,128)(2,1)} %copy-done.6) | copy-start | bytes 786436 | tf_op jit(solution)/shard_map/while
  597.9 3.9 copy-start.6
  615.3 15.0 %copy-start.7 = (bf16[1,512,256]{1,2,0:T(8,128)(2,1)S(1)}, bf16[1,512,256]{1,2,0:T(8,128)(2,1)}, u32[]{:S(2)}) copy-start(bf16[1,512,256]{1,2,0:T(8,128)(2,1)} %copy-done.6) | copy-start | bytes 786436 | tf_op jit(solution)/shard_map/while
  658.4 8.0 copy-start.12
  658.4 8.0 copy-start.13
  685.6 6.1 copy-start.8
  685.7 111.9 %all-to-all-start.3 = ((bf16[32,512,256]{2,1,0:T(8,128)(2,1)}), bf16[32,512,256]{2,1,0:T(8,128)(2,1)}, u32[]{:S(2)}, u32[]{:S(2)}) async-start(bf16[32,512,256]{2,1,0:T(8,128)(2,1)} %copy.174), calls=%async_computation.3 | async-start | bytes 16777216 | tf_op jit(solution)/shard_map/all_to_all | solution.py:155
  716.6 86.2 %copy-start.9 = (f32[4,512,256]{1,2,0:T(8,128)S(1)}, f32[4,512,256]{1,2,0:T(8,128)}, u32[]{:S(2)}) copy-start(f32[4,512,256]{1,2,0:T(8,128)} %get-tuple-element.283) | copy-start | bytes 6291460
  797.5 190.6 %all-to-all-start.4 = ((bf16[32,512,256]{2,1,0:T(8,128)(2,1)}), bf16[32,512,256]{2,1,0:T(8,128)(2,1)}, u32[]{:S(2)}, u32[]{:S(2)}) async-start(bf16[32,512,256]{2,1,0:T(8,128)(2,1)} %copy.180), calls=%async_computation.4 | async-start | bytes 16777216 | tf_op jit(solution)/shard_map/all_to_all | solution.py:156
  802.5 173.4 %all-reduce.5.cloned.1.call-start = ((), (), s32[]{:S(2)}) async-start(), calls=%async_computation.5 | async-start | bytes 2097152 | tf_op jit(solution)/shard_map/psum | solution.py:165
  803.9 174.5 %copy-start.11 = (bf16[32,4]{0,1:T(4,128)(2,1)S(1)}, bf16[32,4]{0,1:T(4,128)(2,1)}, u32[]{:S(2)}) copy-start(bf16[32,4]{0,1:T(4,128)(2,1)} %copy-done.10) | copy-start | bytes 772
  803.9 174.5 %copy-start.15 = (f32[4,512,256]{2,0,1:T(4,128)S(1)}, f32[4,512,256]{2,0,1:T(4,128)}, u32[]{:S(2)}) copy-start(f32[4,512,256]{2,0,1:T(4,128)} %get-tuple-element.281) | copy-start | bytes 6291460
  (17 other events, 29.6 us)
Sparse Core Ops, SparseCore 0:
  155.0 166.1 all-reduce.6
  807.6 168.2 all-reduce.4
where the time goes:
time: 1020 us; the launch traced here: 1010 us
  waiting for transfers between devices  493 us (48%)
  local copies, waits for them, and re-layouts  304 us (30%)
  matrix products  138 us (14%)
  starting transfers between devices  29.5 us (3%)
  other arithmetic  22.2 us (2%)
  between operations  14.8 us (1%)
    psum x1, waiting for transfers between devices, body(): lax.psum((jnp.sum(first_keys, axis=0), jnp.sum(first_values, axis=0)), 's...  169 us
    psum x1, waiting for transfers between devices, from_root(): return lax.psum(kept, axis)  153 us
    dynamic_update_slice x32, local copies, waits for them, and re-layouts, body(): lax.map(one_block, (query_blocks, grad_blocks, logsum, delta, key_blocks,...  130 us
    all_to_all x1, waiting for transfers between devices, body(): lax.all_to_all(send_keys, 'seq', split_axis=0, concat_axis=0, tiled=True)  89.6 us
    all_to_all x1, waiting for transfers between devices, body(): lax.all_to_all(back_keys, 'seq', split_axis=0, concat_axis=0, tiled=True)  80.9 us
    dot_general x4, matrix products, block_terms(): jnp.einsum('ihd,bjhd->hibj', grad_heads, value_heads, preferred_element_t...  27.8 us
    dot_general x4, matrix products, block_terms(): jnp.einsum('hibj,ihd->bjhd', weights_low, grad_heads, preferred_element_t...  23.7 us
    dot_general x4, matrix products, block_terms(): jnp.einsum('ihd,bjhd->hibj', query_heads, key_heads, preferred_element_ty...  22.4 us
  transfers between devices with their start and end apart: 7, of which 4 were waited for; matrix products, arithmetic and copies ran while one was open for 9% of the time, Pallas kernels for 0%

commit v1 on v0

v1 whole, which is shorter than its diff:
```python
import functools
import math

import jax
import jax.numpy as jnp
from jax import lax
from jax.experimental import pallas as pl
from jax.experimental.pallas import tpu as pltpu
from jax.sharding import PartitionSpec as P

MESH = pl.DeviceIdType.MESH
BLOCK = 512
HD = 128
WIDTH = 256
BLK_DEV = 4
RING = 4
NSLOT = 33
FIRST = 32
LOG2E = math.log2(math.e)
MIB = 1024 * 1024


def place():
    seq = lax.axis_index("seq")
    return lax.div(seq, 8), lax.rem(lax.div(seq, 2), 4), lax.rem(seq, 2), lax.axis_index("head")


def device(z, y, c, x):
    return ((z * 4 + y) * 2 + c, x)


def after(index, step):
    return lax.rem(index + step, RING)


def neighbours(z, y, c, x):
    return {
        "sib": device(z, y, 1 - c, x),
        "zr": device(after(z, 1), y, c, x),
        "zl": device(after(z, 3), y, c, x),
        "yr": device(z, after(y, 1), c, x),
        "yl": device(z, after(y, 3), c, x),
    }


def greet(devices):
    barrier = pltpu.get_barrier_semaphore()
    for target in devices:
        pl.semaphore_signal(barrier, inc=1, device_id=target, device_id_type=MESH)
    pl.semaphore_wait(barrier, len(devices))


def gather_kernel(
    keys, values, query, d_out, output, logsum,
    kg, vg, qg, gg, sg,
    grad, outv, stats, send, recv, local,
):
    z, y, c, x = place()
    near = neighbours(z, y, c, x)
    others = [((z * 4 + y) * 2 + c, after(x, step)) for step in (1, 2, 3)]
    greet(list(near.values()) + others)
    started = []

    def remote(index, src, dst, target):
        return pltpu.make_async_remote_copy(
            src_ref=src, dst_ref=dst, send_sem=send.at[index], recv_sem=recv.at[index],
            device_id=target, device_id_type=MESH,
        )

    def go(index, src, dst, target):
        copy = remote(index, src, dst, target)
        copy.start()
        started.append(copy)
        return copy

    def column(z_at, c_at):
        return pl.ds((z_at * 2 + c_at) * BLK_DEV, BLK_DEV)

    def row(y_at):
        return pl.ds(y_at * BLK_DEV, BLK_DEV)

    zl, zr, zo = after(z, 3), after(z, 1), after(z, 2)
    yl, yr = after(y, 3), after(y, 1)
    root = (z == 0) & (y == 0) & (c == 0)
    for step in (1, 2, 3):
        to = after(x, step)
        go(
            22 + step,
            d_out.at[:, pl.ds(pl.multiple_of(to * WIDTH, WIDTH), WIDTH)],
            grad.at[x],
            others[step - 1],
        )
    locals_ = [
        pltpu.make_async_copy(
            d_out.at[:, pl.ds(pl.multiple_of(x * WIDTH, WIDTH), WIDTH)], grad.at[x], local.at[0]
        ),
        pltpu.make_async_copy(output, outv, local.at[1]),
        pltpu.make_async_copy(keys, kg.at[column(z, c)], local.at[2]),
        pltpu.make_async_copy(values, vg.at[column(z, c)], local.at[3]),
        pltpu.make_async_copy(query, qg.at[row(y)], local.at[4]),
    ]
    for copy in locals_:
        copy.start()
    first_own = [
        pltpu.make_async_copy(keys.at[0], kg.at[FIRST], local.at[5]),
        pltpu.make_async_copy(values.at[0], vg.at[FIRST], local.at[6]),
    ]

    @pl.when(root)
    def _():
        for copy in first_own:
            copy.start()
        for copy in first_own:
            copy.wait()

    def first_copies(slot, target):
        return [
            pltpu.make_async_remote_copy(
                src_ref=ref.at[FIRST], dst_ref=ref.at[FIRST],
                send_sem=send.at[28 + 2 * slot + part], recv_sem=recv.at[26 + part],
                device_id=target, device_id_type=MESH,
            )
            for part, ref in enumerate((kg, vg))
        ]

    first_sends = [
        ((z == 0) & (c == 0) & (y <= 1), first_copies(0, near["yr"])),
        ((z == 0) & (c == 0) & (y == 0), first_copies(1, near["yl"])),
        ((c == 0) & (z <= 1), first_copies(2, near["zr"])),
        ((c == 0) & (z == 0), first_copies(3, near["zl"])),
        (c == 0, first_copies(4, near["sib"])),
    ]

    def send_first():
        for condition, copies in first_sends:
            @pl.when(condition)
            def _(copies=copies):
                for copy in copies:
                    copy.start()

    @pl.when(root)
    def _():
        send_first()

    own = column(z, c)
    go(0, keys, kg.at[own], near["zr"])
    go(1, values, vg.at[own], near["zl"])
    go(2, values, vg.at[own], near["zr"])
    go(3, keys, kg.at[own], near["zl"])
    go(4, keys, kg.at[own], near["sib"])
    go(5, values, vg.at[own], near["sib"])
    go(14, query, qg.at[row(y)], near["yr"])
    go(15, query, qg.at[row(y)], near["yl"])

    locals_[0].wait()
    locals_[1].wait()
    for step in (1, 2, 3):
        remote(22 + step, grad.at[x], grad.at[x], others[step - 1]).wait_recv()
    go(16, grad, gg.at[row(y)], near["yl"])
    go(17, grad, gg.at[row(y)], near["yr"])
    keep = pltpu.make_async_copy(grad, gg.at[row(y)], local.at[7])
    keep.start()
    ones = jnp.ones((8, HD), jnp.bfloat16)
    contract = (((1,), (1,)), ((), ()))
    stats[...] = jnp.zeros_like(stats)
    for block in range(BLK_DEV):
        for head in range(2):
            part = pl.ds(head * HD, HD)
            product = grad[block, :, part].astype(jnp.float32) * outv[block, :, part].astype(jnp.float32)
            high = product.astype(jnp.bfloat16)
            low = (product - high.astype(jnp.float32)).astype(jnp.bfloat16)
            total = lax.dot_general(ones, high, contract, preferred_element_type=jnp.float32)
            total += lax.dot_general(ones, low, contract, preferred_element_type=jnp.float32)
            stats[block, pl.ds(2 + head, 1), :] = total[0:1]
            stats[block, pl.ds(head, 1), :] = (
                logsum[pl.ds(head, 1), pl.ds(block * BLOCK, BLOCK)] * LOG2E
            )
    go(18, stats, sg.at[row(y)], near["yr"])
    go(19, stats, sg.at[row(y)], near["yl"])
    keep_stats = pltpu.make_async_copy(stats, sg.at[row(y)], local.at[8])
    keep_stats.start()

    @pl.when(jnp.logical_not(root))
    def _():
        for copy in first_copies(0, near["sib"]):
            copy.wait_recv()
        send_first()

    def arrived(index, ref, piece, source):
        remote(index, ref.at[piece], ref.at[piece], source).wait_recv()

    def forward(index, ref, piece, target):
        go(index, ref.at[piece], ref.at[piece], target)

    left_k, right_k = column(zl, c), column(zr, c)
    arrived(0, kg, left_k, near["zl"])
    forward(6, kg, left_k, near["zr"])
    forward(8, kg, left_k, near["sib"])
    arrived(1, vg, right_k, near["zr"])
    forward(7, vg, right_k, near["zl"])
    forward(9, vg, right_k, near["sib"])
    arrived(14, qg, row(yl), near["yl"])
    forward(20, qg, row(yl), near["yr"])
    arrived(16, gg, row(yr), near["yr"])
    forward(21, gg, row(yr), near["yl"])
    arrived(18, sg, row(yl), near["yl"])
    forward(22, sg, row(yl), near["yr"])
    arrived(2, vg, left_k, near["zl"])
    forward(10, vg, left_k, near["sib"])
    arrived(3, kg, right_k, near["zr"])
    forward(11, kg, right_k, near["sib"])
    far_k = column(zo, c)
    arrived(6, kg, far_k, near["zl"])
    forward(12, kg, far_k, near["sib"])
    arrived(7, vg, far_k, near["zr"])
    forward(13, vg, far_k, near["sib"])
    arrived(15, qg, row(yr), near["yr"])
    arrived(17, gg, row(yl), near["yl"])
    arrived(19, sg, row(yr), near["yr"])
    arrived(20, qg, row(after(y, 2)), near["yl"])
    arrived(21, gg, row(after(y, 2)), near["yr"])
    arrived(22, sg, row(after(y, 2)), near["yl"])
    for index, ref, z_at in (
        (4, kg, z), (5, vg, z), (8, kg, zl), (9, vg, zr),
        (10, vg, zl), (11, kg, zr), (12, kg, zo), (13, vg, zo),
    ):
        arrived(index, ref, column(z_at, 1 - c), near["sib"])
    for copy in locals_[2:] + [keep, keep_stats]:
        copy.wait()
    for copy in started:
        copy.wait_send()
    for condition, copies in first_sends:
        @pl.when(condition)
        def _(copies=copies):
            for copy in copies:
                copy.wait_send()


def pair_kernel(
    selected, kg, vg, qg, gg, sg,
    pk, pv, pq,
    table, items, kbuf, vbuf, qbuf, gbuf, dq, dk, dv, kout, vout, qout, zero,
    in_sem, out_sem, q_sem, zero_sem,
):
    z, y, c, _ = place()
    scale = 1.0 / math.sqrt(HD)

    def clear(at, carry):
        table[at] = 0
        return carry

    lax.fori_loop(0, NSLOT * 4, clear, 0)
    for yq in range(4):
        def enter(at, carry, yq=yq):
            block = lax.div(at, 3)
            chosen = selected[(((z * 4 + yq) * 2 + c) * BLK_DEV + block) * 3 + lax.rem(at, 3)]
            owner = lax.div(chosen, BLK_DEV)
            here = (chosen > 0) & (lax.rem(lax.div(owner, 2), 4) == y)
            slot = (lax.div(owner, 8) * 2 + lax.rem(owner, 2)) * BLK_DEV + lax.rem(chosen, BLK_DEV)

            @pl.when(here)
            def _():
                table[slot * 4 + yq] = 1 + yq * BLK_DEV + block
            return carry

        lax.fori_loop(0, BLK_DEV * 3, enter, 0)
    for block in range(BLK_DEV):
        mine = (z * 2 + c) * BLK_DEV + block
        table[mine * 4 + y] = 1 + y * BLK_DEV + block + 64
        later = ((z * 4 + y) * 2 + c) * BLK_DEV + block > 0
        table[FIRST * 4 + block] = jnp.where(later, 1 + y * BLK_DEV + block, 0)

    def compact(at, count):
        entry = table[at]
        items[count] = at * 128 + entry
        return count + jnp.where(entry > 0, 1, 0)

    count = lax.fori_loop(0, NSLOT * 4, compact, 0)
    items[count] = -1

    zero[...] = jnp.zeros_like(zero)

    def idle(slot):
        return (
            table[slot * 4] + table[slot * 4 + 1] + table[slot * 4 + 2] + table[slot * 4 + 3]
        ) == 0

    def blank(slot):
        return [
            pltpu.make_async_copy(zero, ref.at[slot], zero_sem.at[slot, part])
            for part, ref in enumerate((pk, pv))
        ]

    def start_blank(slot, carry):
        @pl.when(idle(slot))
        def _():
            for copy in blank(slot):
                copy.start()
        return carry

    lax.fori_loop(0, NSLOT, start_blank, 0)

    def decode(item):
        slot = lax.div(item, 512)
        entry = lax.rem(item, 128) - 1
        return slot, lax.rem(entry, 64), entry >= 64

    def loads(at):
        slot, block, _ = decode(items[at])
        side = lax.rem(at, 2)
        return [
            pltpu.make_async_copy(kg.at[slot], kbuf.at[side], in_sem.at[side, 0]),
            pltpu.make_async_copy(vg.at[slot], vbuf.at[side], in_sem.at[side, 1]),
            pltpu.make_async_copy(qg.at[block], qbuf.at[side], in_sem.at[side, 2]),
            pltpu.make_async_copy(gg.at[block], gbuf.at[side], in_sem.at[side, 3]),
        ]

    for copy in loads(0):
        copy.start()
    dq[...] = jnp.zeros_like(dq)

    nt = (((1,), (1,)), ((), ()))
    nn = (((1,), (0,)), ((), ()))
    tn = (((0,), (0,)), ((), ()))

    def dot(a, b, dims):
        return lax.dot_general(a, b, dims, preferred_element_type=jnp.float32)

    def work(side, block, causal):
        for head in range(2):
            part = pl.ds(head * HD, HD)
            k, v = kbuf[side, :, part], vbuf[side, :, part]
            q, g = qbuf[side, :, part], gbuf[side, :, part]
            lse = sg[block, pl.ds(head, 1), :]
            delta = sg[block, pl.ds(2 + head, 1), :]
            p = jnp.exp2(dot(k, q, nt) * (scale * LOG2E) - lse)
            if causal:
                key_at = lax.broadcasted_iota(jnp.int32, (BLOCK, BLOCK), 0)
                query_at = lax.broadcasted_iota(jnp.int32, (BLOCK, BLOCK), 1)
                p = jnp.where(key_at <= query_at, p, 0.0)
            ds = (p * (dot(v, g, nt) - delta)).astype(jnp.bfloat16)
            dv[:, part] += dot(p.astype(jnp.bfloat16), g, nn)
            dk[:, part] += dot(ds, q, nn)
            dq[block, :, part] += dot(ds, k, tn)

    outs = [
        pltpu.make_async_copy(kout, pk.at[0], out_sem.at[0]),
        pltpu.make_async_copy(vout, pv.at[0], out_sem.at[1]),
    ]

    def item_step(at, carry):
        opened, written = carry
        slot, block, causal = decode(items[at])
        following = items[at + 1]
        side = lax.rem(at, 2)

        @pl.when(following >= 0)
        def _():
            for copy in loads(at + 1):
                copy.start()

        for copy in loads(at):
            copy.wait()

        @pl.when(slot != opened)
        def _():
            dk[...] = jnp.zeros_like(dk)
            dv[...] = jnp.zeros_like(dv)

        @pl.when(causal)
        def _():
            work(side, block, True)

        @pl.when(jnp.logical_not(causal))
        def _():
            work(side, block, False)

        closing = (following < 0) | (lax.div(following, 512) != slot)

        @pl.when(closing)
        def _():
            @pl.when(written > 0)
            def _():
                for copy in outs:
                    copy.wait()
            kout[...] = (dk[...] * scale).astype(jnp.bfloat16)
            vout[...] = dv[...].astype(jnp.bfloat16)
            pltpu.make_async_copy(kout, pk.at[slot], out_sem.at[0]).start()
            pltpu.make_async_copy(vout, pv.at[slot], out_sem.at[1]).start()

        return slot, written + jnp.where(closing, 1, 0)

    lax.fori_loop(0, count, item_step, (-1, 0))

    def finish(block, carry):
        qout[block] = (dq[block] * scale).astype(jnp.bfloat16)
        pltpu.make_async_copy(qout.at[block], pq.at[block], q_sem.at[block]).start()
        return carry

    lax.fori_loop(0, 16, finish, 0)
    for copy in outs:
        copy.wait()

    def drain(block, carry):
        pltpu.make_async_copy(qout.at[block], pq.at[block], q_sem.at[block]).wait()
        return carry

    lax.fori_loop(0, 16, drain, 0)

    def wait_blank(slot, carry):
        @pl.when(idle(slot))
        def _():
            for copy in blank(slot):
                copy.wait()
        return carry

    lax.fori_loop(0, NSLOT, wait_blank, 0)


def scatter_kernel(
    pk, pv, pq,
    out_q, out_k, out_v,
    ownk, ownv, sibk, sibv, relk, relv, fink, finv,
    ownq, relq, finq, fown, frecv, fsum, fsend,
    send, recv, local,
):
    z, y, c, x = place()
    near = neighbours(z, y, c, x)
    greet(list(near.values()))
    started = []

    def remote(index, src, dst, target):
        return pltpu.make_async_remote_copy(
            src_ref=src, dst_ref=dst, send_sem=send.at[index], recv_sem=recv.at[index],
            device_id=target, device_id_type=MESH,
        )

    def go(index, src, dst, target):
        copy = remote(index, src, dst, target)
        copy.start()
        started.append(copy)

    def came(index, dst):
        remote(index, dst, dst, near["sib"]).wait_recv()

    def column(z_at, c_at):
        return pl.ds((z_at * 2 + c_at) * BLK_DEV, BLK_DEV)

    hops = (2, 1, 3, 0)
    parts = ((pk, ownk, sibk), (pv, ownv, sibv))
    locals_k = []
    for j, hop in enumerate(hops):
        for part, (ref, held, other) in enumerate(parts):
            go(2 * j + part, ref.at[column(after(z, hop), 1 - c)], other.at[j], near["sib"])
            copy = pltpu.make_async_copy(
                ref.at[column(after(z, hop), c)], held.at[j], local.at[2 * j + part]
            )
            copy.start()
            locals_k.append(copy)
        if j == 0:
            locals_q = []
            for jq, hop_q in enumerate(hops):
                copy = pltpu.make_async_copy(
                    pq.at[pl.ds(after(y, hop_q) * BLK_DEV, BLK_DEV)], ownq.at[jq], local.at[8 + jq]
                )
                copy.start()
                locals_q.append(copy)
            locals_f = [
                pltpu.make_async_copy(ref.at[FIRST], fown.at[part], local.at[12 + part])
                for part, ref in enumerate((pk, pv))
            ]
            for copy in locals_f:
                copy.start()

    def add(dst, src, blocks):
        def one(block, carry):
            dst[block] = (dst[block].astype(jnp.float32) + src[block].astype(jnp.float32)).astype(
                jnp.bfloat16
            )
            return carry

        lax.fori_loop(blocks[0], blocks[1], one, 0)

    def merge(j, part):
        _, held, other = parts[part]
        locals_k[2 * j + part].wait()
        came(2 * j + part, other.at[j])
        add(held.at[j], other.at[j], (0, BLK_DEV))

    locals_q[0].wait()
    go(8, ownq.at[0, pl.ds(0, 2)], relq.at[0], near["yr"])
    go(9, ownq.at[0, pl.ds(2, 2)], relq.at[1], near["yl"])
    locals_q[1].wait()
    go(10, ownq.at[1, pl.ds(2, 2)], finq.at[0, pl.ds(2, 2)], near["yr"])
    locals_q[2].wait()
    go(11, ownq.at[2, pl.ds(0, 2)], finq.at[1, pl.ds(0, 2)], near["yl"])

    merge(0, 0)
    go(14, ownk.at[0], relk, near["zr"])
    merge(0, 1)
    go(15, ownv.at[0], relv, near["zl"])
    merge(1, 1)
    go(16, ownv.at[1], finv.at[0], near["zr"])
    merge(2, 0)
    go(17, ownk.at[2], fink.at[1], near["zl"])

    for copy in locals_f:
        copy.wait()

    def f_copy(send_at, recv_at, src, dst, target):
        return pltpu.make_async_remote_copy(
            src_ref=src, dst_ref=dst, send_sem=send.at[send_at], recv_sem=recv.at[recv_at],
            device_id=target, device_id_type=MESH,
        )

    to_sib = f_copy(20, 20, fown, frecv.at[0], near["sib"])
    steps = [
        ((c == 0) & ((y == 2) | (y == 1)), f_copy(21, 21, fsend.at[0], frecv.at[1], near["yl"])),
        ((c == 0) & (y == 3), f_copy(22, 22, fsend.at[0], frecv.at[2], near["yr"])),
        ((c == 0) & (y == 0) & ((z == 2) | (z == 1)), f_copy(23, 23, fsend.at[1], frecv.at[3], near["zl"])),
        ((c == 0) & (y == 0) & (z == 3), f_copy(24, 24, fsend.at[1], frecv.at[4], near["zr"])),
    ]
    gets = [
        (c == 0) & ((y == 1) | (y == 0)),
        (c == 0) & (y == 0),
        (c == 0) & (y == 0) & ((z == 1) | (z == 0)),
        (c == 0) & (y == 0) & (z == 0),
    ]

    def f_take(at):
        fsum[...] += frecv[at].astype(jnp.float32)

    @pl.when(c == 1)
    def _():
        to_sib.start()

    @pl.when(c == 0)
    def _():
        to_sib.wait_recv()
        fsum[...] = fown[...].astype(jnp.float32) + frecv[0].astype(jnp.float32)

    for step in range(2):
        @pl.when(gets[step])
        def _(step=step):
            steps[step][1].wait_recv()
            f_take(1 + step)

    @pl.when((c == 0) & (y > 0))
    def _():
        fsend[0] = fsum[...].astype(jnp.bfloat16)

    for step in range(2):
        @pl.when(steps[step][0])
        def _(step=step):
            steps[step][1].start()

    merge(1, 0)
    came(14, relk)
    add(ownk.at[1], relk, (0, BLK_DEV))
    go(18, ownk.at[1], fink.at[0], near["zr"])
    merge(2, 1)
    came(15, relv)
    add(ownv.at[2], relv, (0, BLK_DEV))
    go(19, ownv.at[2], finv.at[1], near["zl"])

    came(8, relq.at[0])
    add(ownq.at[1], relq.at[0], (0, 2))
    go(12, ownq.at[1, pl.ds(0, 2)], finq.at[0, pl.ds(0, 2)], near["yr"])
    came(9, relq.at[1])

    def add_high(block, carry):
        ownq[2, block + 2] = (
            ownq[2, block + 2].astype(jnp.float32) + relq[1, block].astype(jnp.float32)
        ).astype(jnp.bfloat16)
        return carry

    lax.fori_loop(0, 2, add_high, 0)
    go(13, ownq.at[2, pl.ds(2, 2)], finq.at[1, pl.ds(2, 2)], near["yl"])

    for step in (2, 3):
        @pl.when(gets[step])
        def _(step=step):
            steps[step][1].wait_recv()
            f_take(1 + step)

    @pl.when((c == 0) & (y == 0) & (z > 0))
    def _():
        fsend[1] = fsum[...].astype(jnp.bfloat16)

    for step in (2, 3):
        @pl.when(steps[step][0])
        def _(step=step):
            steps[step][1].start()

    locals_q[3].wait()
    came(10, finq.at[0, pl.ds(2, 2)])
    came(11, finq.at[1, pl.ds(0, 2)])
    came(12, finq.at[0, pl.ds(0, 2)])
    came(13, finq.at[1, pl.ds(2, 2)])

    def total(held, parts_in, out):
        def one(block, carry):
            value = held[block].astype(jnp.float32)
            for ref in parts_in:
                value += ref[block].astype(jnp.float32)
            out[block] = value.astype(jnp.bfloat16)
            return carry

        return one

    lax.fori_loop(0, BLK_DEV, total(ownq.at[3], (finq.at[0], finq.at[1]), out_q), 0)

    root = (z == 0) & (y == 0) & (c == 0)
    for part, (held, other, fin, out) in enumerate(
        ((ownk, sibk, fink, out_k), (ownv, sibv, finv, out_v))
    ):
        locals_k[6 + part].wait()
        came(6 + part, other.at[3])
        came((18, 16)[part], fin.at[0])
        came((17, 19)[part], fin.at[1])
        ins = (other.at[3], fin.at[0], fin.at[1])
        lax.fori_loop(1, BLK_DEV, total(held.at[3], ins, out), 0)
        value = held[3, 0].astype(jnp.float32)
        for ref in ins:
            value += ref[0].astype(jnp.float32)

        @pl.when(root)
        def _(value=value, out=out, part=part):
            out[0] = (value + fsum[part]).astype(jnp.bfloat16)

        @pl.when(jnp.logical_not(root))
        def _(value=value, out=out):
            out[0] = value.astype(jnp.bfloat16)

    for copy in started:
        copy.wait_send()

    @pl.when(c == 1)
    def _():
        to_sib.wait_send()

    for condition, copy in steps:
        @pl.when(condition)
        def _(copy=copy):
            copy.wait_send()


def body(query, keys, values, output, d_out, row_logsum, selected):
    bf16, f32 = jnp.bfloat16, jnp.float32
    any_spec = pl.BlockSpec(memory_space=pl.ANY)
    vmem_spec = pl.BlockSpec(memory_space=pltpu.VMEM)
    smem_spec = pl.BlockSpec(memory_space=pltpu.SMEM)
    blocked = (BLK_DEV, BLOCK, WIDTH)
    shape = jax.ShapeDtypeStruct
    dma, vmem, smem = pltpu.SemaphoreType.DMA, pltpu.VMEM, pltpu.SMEM
    kg, vg, qg, gg, sg = pl.pallas_call(
        gather_kernel,
        out_shape=[
            shape((NSLOT, BLOCK, WIDTH), bf16),
            shape((NSLOT, BLOCK, WIDTH), bf16),
            shape((16, BLOCK, WIDTH), bf16),
            shape((16, BLOCK, WIDTH), bf16),
            shape((16, 8, BLOCK), f32),
        ],
        in_specs=[any_spec] * 5 + [vmem_spec],
        out_specs=[any_spec] * 5,
        scratch_shapes=[
            vmem(blocked, bf16),
            vmem(blocked, bf16),
            vmem((BLK_DEV, 8, BLOCK), f32),
            dma((38,)),
            dma((28,)),
            dma((9,)),
        ],
        compiler_params=pltpu.CompilerParams(
            collective_id=0, has_side_effects=True, vmem_limit_bytes=32 * MIB
        ),
        name="gather",
    )(
        keys.reshape(blocked), values.reshape(blocked), query.reshape(blocked),
        d_out, output.reshape(blocked), row_logsum,
    )
    pk, pv, pq = pl.pallas_call(
        pair_kernel,
        out_shape=[
            shape((NSLOT, BLOCK, WIDTH), bf16),
            shape((NSLOT, BLOCK, WIDTH), bf16),
            shape((16, BLOCK, WIDTH), bf16),
        ],
        in_specs=[smem_spec] + [any_spec] * 4 + [vmem_spec],
        out_specs=[any_spec] * 3,
        scratch_shapes=[
            smem((NSLOT * 4,), jnp.int32),
            smem((NSLOT * 4 + 1,), jnp.int32),
            vmem((2, BLOCK, WIDTH), bf16),
            vmem((2, BLOCK, WIDTH), bf16),
            vmem((2, BLOCK, WIDTH), bf16),
            vmem((2, BLOCK, WIDTH), bf16),
            vmem((16, BLOCK, WIDTH), f32),
            vmem((BLOCK, WIDTH), f32),
            vmem((BLOCK, WIDTH), f32),
            vmem((BLOCK, WIDTH), bf16),
            vmem((BLOCK, WIDTH), bf16),
            vmem((16, BLOCK, WIDTH), bf16),
            vmem((BLOCK, WIDTH), bf16),
            dma((2, 4)),
            dma((2,)),
            dma((16,)),
            dma((NSLOT, 2)),
        ],
        compiler_params=pltpu.CompilerParams(vmem_limit_bytes=48 * MIB),
        name="pairs",
    )(selected.reshape(-1), kg, vg, qg, gg, sg)
    out_q, out_k, out_v = pl.pallas_call(
        scatter_kernel,
        out_shape=[shape(blocked, bf16)] * 3,
        in_specs=[any_spec] * 3,
        out_specs=[vmem_spec] * 3,
        scratch_shapes=[
            vmem((4,) + blocked, bf16),
            vmem((4,) + blocked, bf16),
            vmem((4,) + blocked, bf16),
            vmem((4,) + blocked, bf16),
            vmem(blocked, bf16),
            vmem(blocked, bf16),
            vmem((2,) + blocked, bf16),
            vmem((2,) + blocked, bf16),
            vmem((4,) + blocked, bf16),
            vmem((2, 2, BLOCK, WIDTH), bf16),
            vmem((2,) + blocked, bf16),
            vmem((2, BLOCK, WIDTH), bf16),
            vmem((5, 2, BLOCK, WIDTH), bf16),
            vmem((2, BLOCK, WIDTH), f32),
            vmem((2, 2, BLOCK, WIDTH), bf16),
            dma((25,)),
            dma((25,)),
            dma((14,)),
        ],
        compiler_params=pltpu.CompilerParams(
            collective_id=1, has_side_effects=True, vmem_limit_bytes=56 * MIB
        ),
        name="scatter",
    )(pk, pv, pq)
    flat = (BLK_DEV * BLOCK, WIDTH)
    return out_q.reshape(flat), out_k.reshape(flat), out_v.reshape(flat)


def solution(mesh):
    in_specs = (
        P("seq", "head"),
        P("seq", "head"),
        P("seq", "head"),
        P("seq", "head"),
        P(("seq", "head"), None),
        P("head", "seq"),
        P(),
    )
    out_specs = (P("seq", "head"), P("seq", "head"), P("seq", "head"))
    return jax.shard_map(body, mesh=mesh, in_specs=in_specs, out_specs=out_specs, check_vma=False)
```

time: 1020 us -> 283 us (0.28); the launches traced: 1010 us -> 282 us
  waiting for transfers between devices: 493 us -> 0 us
  local copies, waits for them, and re-layouts: 304 us -> 24 us
  Pallas kernels: 0 us -> 257 us
  matrix products: 138 us -> 0 us
  starting transfers between devices: 29.5 us -> 0 us
  other arithmetic: 22.2 us -> 0 us
  between operations: 14.8 us -> 0.69 us
    psum x2 -> x0, waiting for transfers between devices: 323 us -> none  [the longest x1 169 us: body(): lax.psum((jnp.sum(first_keys, axis=0), jnp.sum(first_values, axis=0)), 's...]
    pallas_call x0 -> x3, Pallas kernels: none -> 257 us  [the longest x1 146 us: body(): pl.pallas_call(scatter_kernel, out_shape=[shape(blocked, bf16)] * 3, in_s...]
    all_to_all x5 -> x0, waiting for transfers between devices: 171 us -> none  [the longest x1 89.6 us: body(): lax.all_to_all(send_keys, 'seq', split_axis=0, concat_axis=0, tiled=True)]
    dot_general x26 -> x0, matrix products: 138 us -> none  [the longest x4 27.8 us: block_terms(): jnp.einsum('ihd,bjhd->hibj', grad_heads, value_heads, preferred_element_t...]
    dynamic_update_slice x32 -> x0, local copies, waits for them, and re-layouts: 130 us -> none  [body(): lax.map(one_block, (query_blocks, grad_blocks, logsum, delta, key_blocks,...]
    convert_element_type x7 -> x0, local copies, waits for them, and re-layouts: 49.9 us -> none  [the longest x1 11.5 us: body(): send_keys = jnp.einsum('rb,bte->rte', route_low, key_blocks, preferred_el...]
    gather x8 -> x0, local copies, waits for them, and re-layouts: 31.9 us -> none  [the longest x4 16 us: one_block(): picked_values = jnp.take(got_values, sources, axis=0)]
    all_to_all x5 -> x0, starting transfers between devices: 29.2 us -> none  [the longest x1 8.81 us: body(): lax.all_to_all(send_keys, 'seq', split_axis=0, concat_axis=0, tiled=True)]
  transfers between devices with their start and end apart: 7 -> 0, of which waited for: 4 -> 0; matrix products, arithmetic and copies ran while one was open for 9% -> 0% of each run, Pallas kernels for 0% -> 0%
where the time goes in v1:
time: 283 us; the launch traced here: 282 us
  Pallas kernels  257 us (91%)
  local copies, waits for them, and re-layouts  24 us (8%)
    pallas_call x1, Pallas kernels, body(): pl.pallas_call(scatter_kernel, out_shape=[shape(blocked, bf16)] * 3, in_s...  146 us
    pallas_call x1, Pallas kernels, body(): pl.pallas_call(gather_kernel, out_shape=[shape((NSLOT, BLOCK, WIDTH), bf1...  80.9 us
    pallas_call x1, Pallas kernels, body(): pl.pallas_call(pair_kernel, out_shape=[shape((NSLOT, BLOCK, WIDTH), bf16)...  30.5 us
    unnamed x24, local copies, waits for them, and re-layouts  23.8 us

profile of v1, /device:TPU:0, one launch (start us, length us, event | category | flops | bytes accessed | tf_op | source)
XLA Modules:
  0.0 281.9 jit_solution(9973115542200908096)
XLA Ops:
  0.6 0.8 copy.10
  1.4 0.2 reshape.30.selected
  1.6 0.0 copy-start.4
  1.6 1.2 copy-done.4
  2.9 0.0 copy-start.5
  2.9 1.2 copy-done.5
  4.1 0.0 copy-start.6
  4.1 1.2 copy-done.6
  5.3 0.0 copy-start.7
  5.3 1.2 copy-done.7
  6.5 1.2 copy-done.8
  7.8 0.7 copy-done.9
  8.5 80.9 %gather.1 = (bf16[33,512,256]{2,1,0:T(8,128)(2,1)S(1)}, bf16[33,512,256]{2,1,0:T(8,128)(2,1)}, bf16[16,512,256]{2,1,0:T(8,128)(2,1)S(1)}, bf16[16,512,256]{2,1,0:T(8,128)(2,1)S(1)}, f32[16,8,512]{2,1,0:T(8,128)S(1)}) custom-call(bf16[4,512,256]{2,1,0:T(8,128)(2,1)S(1)} %bitcast.7, bf16[4,512,256]{2,1,0:T(8,128)(2,1)S(1)} %bitcast.8, ...), custom_call_target="tpu_custom_call" | custom-call | tf_op jit(solution)/shard_map/gather/pallas_call | solution.py:656
  89.4 0.0 copy-start
  89.4 3.3 %copy-done = bf16[33,512,256]{2,1,0:T(8,128)(2,1)} copy-done((bf16[33,512,256]{2,1,0:T(8,128)(2,1)}, bf16[33,512,256]{2,1,0:T(8,128)(2,1)S(1)}, u32[]{:S(2)}) %copy-start) | copy-done | bytes 8650776
  92.7 2.1 copy-done.1
  94.8 2.0 copy-done.2
  96.8 30.5 %pairs.1 = (bf16[33,512,256]{2,1,0:T(8,128)(2,1)}, bf16[33,512,256]{2,1,0:T(8,128)(2,1)}, bf16[16,512,256]{2,1,0:T(8,128)(2,1)S(1)}) custom-call(s32[384]{0:T(512)S(1)} %reshape.30.selected, bf16[33,512,256]{2,1,0:T(8,128)(2,1)} %copy-done, bf16[33,512,256]{2,1,0:T(8,128)(2,1)} %get-tuple-element.15.vg, bf16[16,512,256]{2,1,0:T(8,128)(2,1)} %copy-done.1, ...), custom_call_target="tpu_custom_call" | custom-call | tf_op jit(solution)/shard_map/pairs/pallas_call | solution.py:683
  127.3 0.0 copy-start.3
  127.3 2.0 copy-done.3
  129.2 145.9 %scatter.1 = (bf16[4,512,256]{2,1,0:T(8,128)(2,1)}, bf16[4,512,256]{2,1,0:T(8,128)(2,1)}, bf16[4,512,256]{2,1,0:T(8,128)(2,1)}) custom-call(bf16[33,512,256]{2,1,0:T(8,128)(2,1)} %get-tuple-element.19.pk, bf16[33,512,256]{2,1,0:T(8,128)(2,1)} %get-tuple-element.20.pv, bf16[16,512,256]{2,1,0:T(8,128)(2,1)} %copy-done.3), custom_call_target="tpu_custom_call" | custom-call | tf_op jit(solution)/shard_map/scatter/pallas_call | solution.py:714
  275.1 2.3 copy.14
  277.4 2.3 copy.15
  279.7 2.3 copy.16
  (4 shorter events, 0.0 us)
Async XLA Ops:
  1.6 1.2 copy-start.4
  2.9 1.2 copy-start.5
  4.1 1.2 copy-start.6
  5.3 1.2 copy-start.7
  6.5 1.2 copy-start.8
  7.8 0.7 copy-start.9
  89.4 3.3 %copy-start = (bf16[33,512,256]{2,1,0:T(8,128)(2,1)}, bf16[33,512,256]{2,1,0:T(8,128)(2,1)S(1)}, u32[]{:S(2)}) copy-start(bf16[33,512,256]{2,1,0:T(8,128)(2,1)S(1)} %get-tuple-element.14.kg) | copy-start | bytes 25952260
  92.7 2.1 copy-start.1
  94.8 2.0 copy-start.2
  127.3 2.0 copy-start.3

commit v2 on v1

v2 whole, which is shorter than its diff:
```python
import functools
import math

import jax
import jax.numpy as jnp
from jax import lax
from jax.experimental import pallas as pl
from jax.experimental.pallas import tpu as pltpu
from jax.sharding import PartitionSpec as P

MESH = pl.DeviceIdType.MESH
BLOCK = 512
HD = 128
WIDTH = 256
BLK_DEV = 4
RING = 4
NSLOT = 33
FIRST = 32
LOG2E = math.log2(math.e)
VMEM = 60 * 1024 * 1024


def place():
    seq = lax.axis_index("seq")
    return lax.div(seq, 8), lax.rem(lax.div(seq, 2), 4), lax.rem(seq, 2), lax.axis_index("head")


def device(z, y, c, x):
    return ((z * 4 + y) * 2 + c, x)


def after(index, step):
    return lax.rem(index + step, RING)


def neighbours(z, y, c, x):
    return {
        "sib": device(z, y, 1 - c, x),
        "zr": device(after(z, 1), y, c, x),
        "zl": device(after(z, 3), y, c, x),
        "yr": device(z, after(y, 1), c, x),
        "yl": device(z, after(y, 3), c, x),
    }


def greet(devices):
    barrier = pltpu.get_barrier_semaphore()
    for target in devices:
        pl.semaphore_signal(barrier, inc=1, device_id=target, device_id_type=MESH)
    pl.semaphore_wait(barrier, len(devices))


NT = (((1,), (1,)), ((), ()))
NN = (((1,), (0,)), ((), ()))
TN = (((0,), (0,)), ((), ()))


def dot(a, b, dims):
    return lax.dot_general(a, b, dims, preferred_element_type=jnp.float32)


def gather_kernel(
    keys, values, query, d_out, output, logsum,
    kg, vg, qg, gg, sg, own_q, own_k, own_v,
    grad, outv, kv, vv, qv, stats, accq, acck, accv, send, recv, local,
):
    z, y, c, x = place()
    near = neighbours(z, y, c, x)
    others = [((z * 4 + y) * 2 + c, after(x, step)) for step in (1, 2, 3)]
    greet(list(near.values()) + others)
    started = []

    def remote(index, src, dst, target):
        return pltpu.make_async_remote_copy(
            src_ref=src, dst_ref=dst, send_sem=send.at[index], recv_sem=recv.at[index],
            device_id=target, device_id_type=MESH,
        )

    def go(index, src, dst, target):
        copy = remote(index, src, dst, target)
        copy.start()
        started.append(copy)
        return copy

    def column(z_at, c_at):
        return pl.ds((z_at * 2 + c_at) * BLK_DEV, BLK_DEV)

    def row(y_at):
        return pl.ds(y_at * BLK_DEV, BLK_DEV)

    zl, zr, zo = after(z, 3), after(z, 1), after(z, 2)
    yl, yr = after(y, 3), after(y, 1)
    top = (z == 0) & (y == 0)
    root = top & (c == 0)

    first_own = [
        pltpu.make_async_copy(keys.at[0], kg.at[FIRST], local.at[0]),
        pltpu.make_async_copy(values.at[0], vg.at[FIRST], local.at[1]),
    ]

    def first_copy(ref, send_at, recv_at, target):
        return pltpu.make_async_remote_copy(
            src_ref=ref.at[FIRST], dst_ref=ref.at[FIRST],
            send_sem=send.at[send_at], recv_sem=recv.at[recv_at],
            device_id=target, device_id_type=MESH,
        )

    first_sends = []
    for core, ref in enumerate((kg, vg)):
        mine = c == core
        first_sends += [
            (mine & (z == 0) & (y <= 1), first_copy(ref, 28, 26, near["yr"])),
            (mine & (z == 0) & (y == 0), first_copy(ref, 29, 26, near["yl"])),
            (mine & (z <= 1), first_copy(ref, 30, 26, near["zr"])),
            (mine & (z == 0), first_copy(ref, 31, 26, near["zl"])),
            (mine & jnp.logical_not(top & (c == 1)), first_copy(ref, 32, 27, near["sib"])),
        ]
    first_start = first_copy(vg, 33, 26, near["sib"])

    def send_first():
        for condition, copy in first_sends:
            @pl.when(condition)
            def _(copy=copy):
                copy.start()

    @pl.when(root)
    def _():
        for copy in first_own:
            copy.start()
        for copy in first_own:
            copy.wait()
        first_start.start()
        send_first()

    @pl.when(top & (c == 1))
    def _():
        first_start.wait_recv()
        send_first()

    for step in (1, 2, 3):
        to = after(x, step)
        go(
            22 + step,
            d_out.at[:, pl.ds(pl.multiple_of(to * WIDTH, WIDTH), WIDTH)],
            grad.at[x],
            others[step - 1],
        )
    to_vmem = [
        pltpu.make_async_copy(
            d_out.at[:, pl.ds(pl.multiple_of(x * WIDTH, WIDTH), WIDTH)], grad.at[x], local.at[2]
        ),
        pltpu.make_async_copy(output, outv, local.at[3]),
        pltpu.make_async_copy(keys, kv, local.at[4]),
        pltpu.make_async_copy(values, vv, local.at[5]),
        pltpu.make_async_copy(query, qv, local.at[6]),
    ]
    kept = [
        pltpu.make_async_copy(keys, kg.at[column(z, c)], local.at[7]),
        pltpu.make_async_copy(values, vg.at[column(z, c)], local.at[8]),
        pltpu.make_async_copy(query, qg.at[row(y)], local.at[9]),
    ]
    for copy in to_vmem + kept:
        copy.start()

    own = column(z, c)
    go(0, keys, kg.at[own], near["zr"])
    go(1, values, vg.at[own], near["zl"])
    go(14, query, qg.at[row(y)], near["yr"])
    go(15, query, qg.at[row(y)], near["yl"])
    go(4, keys, kg.at[own], near["sib"])
    go(5, values, vg.at[own], near["sib"])

    to_vmem[0].wait()
    to_vmem[1].wait()
    for step in (1, 2, 3):
        remote(22 + step, grad.at[x], grad.at[x], others[step - 1]).wait_recv()
    go(16, grad, gg.at[row(y)], near["yl"])
    go(17, grad, gg.at[row(y)], near["yr"])
    go(2, values, vg.at[own], near["zr"])
    go(3, keys, kg.at[own], near["zl"])
    kept.append(pltpu.make_async_copy(grad, gg.at[row(y)], local.at[10]))
    kept[-1].start()
    stats[...] = jnp.zeros_like(stats)

    ones = jnp.ones((8, HD), jnp.bfloat16)
    for block in range(BLK_DEV):
        for head in range(2):
            part = pl.ds(head * HD, HD)
            product = grad[block, :, part].astype(jnp.float32) * outv[block, :, part].astype(jnp.float32)
            high = product.astype(jnp.bfloat16)
            low = (product - high.astype(jnp.float32)).astype(jnp.bfloat16)
            total = dot(ones, high, NT) + dot(ones, low, NT)
            stats[block, pl.ds(2 + head, 1), :] = total[0:1]
            stats[block, pl.ds(head, 1), :] = (
                logsum[pl.ds(head, 1), pl.ds(block * BLOCK, BLOCK)] * LOG2E
            )
    go(18, stats, sg.at[row(y)], near["yr"])
    go(19, stats, sg.at[row(y)], near["yl"])
    kept.append(pltpu.make_async_copy(stats, sg.at[row(y)], local.at[11]))
    kept[-1].start()

    @pl.when(jnp.logical_not(top))
    def _():
        first_copy(kg, 28, 26, near["sib"]).wait_recv()
        send_first()

    for copy in to_vmem[2:]:
        copy.wait()
    scale = 1.0 / math.sqrt(HD)

    def own_block(block, carry):
        for head in range(2):
            part = pl.ds(head * HD, HD)
            k, v, q, g = kv[block, :, part], vv[block, :, part], qv[block, :, part], grad[block, :, part]
            lse = stats[block, pl.ds(head, 1), :]
            delta = stats[block, pl.ds(2 + head, 1), :]
            p = jnp.exp2(dot(k, q, NT) * (scale * LOG2E) - lse)
            key_at = lax.broadcasted_iota(jnp.int32, (BLOCK, BLOCK), 0)
            query_at = lax.broadcasted_iota(jnp.int32, (BLOCK, BLOCK), 1)
            p = jnp.where(key_at <= query_at, p, 0.0)
            ds = (p * (dot(v, g, NT) - delta)).astype(jnp.bfloat16)
            accv[block, :, part] = dot(p.astype(jnp.bfloat16), g, NN)
            acck[block, :, part] = dot(ds, q, NN) * scale
            accq[block, :, part] = dot(ds, k, TN) * scale
        return carry

    lax.fori_loop(0, BLK_DEV, own_block, 0)
    for index, (src, dst) in enumerate(((accq, own_q), (acck, own_k), (accv, own_v))):
        kept.append(pltpu.make_async_copy(src, dst, local.at[12 + index]))
        kept[-1].start()

    def arrived(index, ref, piece, source):
        remote(index, ref.at[piece], ref.at[piece], source).wait_recv()

    def forward(index, ref, piece, target):
        go(index, ref.at[piece], ref.at[piece], target)

    left_k, right_k, far_k = column(zl, c), column(zr, c), column(zo, c)
    arrived(0, kg, left_k, near["zl"])
    forward(6, kg, left_k, near["zr"])
    arrived(1, vg, right_k, near["zr"])
    forward(7, vg, right_k, near["zl"])
    arrived(14, qg, row(yl), near["yl"])
    forward(20, qg, row(yl), near["yr"])
    arrived(18, sg, row(yl), near["yl"])
    forward(22, sg, row(yl), near["yr"])
    arrived(16, gg, row(yr), near["yr"])
    forward(21, gg, row(yr), near["yl"])
    forward(8, kg, left_k, near["sib"])
    forward(9, vg, right_k, near["sib"])
    arrived(2, vg, left_k, near["zl"])
    forward(10, vg, left_k, near["sib"])
    arrived(3, kg, right_k, near["zr"])
    forward(11, kg, right_k, near["sib"])
    arrived(6, kg, far_k, near["zl"])
    forward(12, kg, far_k, near["sib"])
    arrived(7, vg, far_k, near["zr"])
    forward(13, vg, far_k, near["sib"])
    arrived(15, qg, row(yr), near["yr"])
    arrived(17, gg, row(yl), near["yl"])
    arrived(19, sg, row(yr), near["yr"])
    arrived(20, qg, row(after(y, 2)), near["yl"])
    arrived(21, gg, row(after(y, 2)), near["yr"])
    arrived(22, sg, row(after(y, 2)), near["yl"])

    @pl.when(jnp.logical_not(root))
    def _():
        first_copy(kg, 32, 27, near["sib"]).wait_recv()

    for index, ref, z_at in (
        (4, kg, z), (5, vg, z), (8, kg, zl), (9, vg, zr),
        (10, vg, zl), (11, kg, zr), (12, kg, zo), (13, vg, zo),
    ):
        arrived(index, ref, column(z_at, 1 - c), near["sib"])
    for copy in kept:
        copy.wait()
    for copy in started:
        copy.wait_send()

    @pl.when(root)
    def _():
        first_start.wait_send()

    for condition, copy in first_sends:
        @pl.when(condition)
        def _(copy=copy):
            copy.wait_send()


def pair_kernel(
    selected, kg, vg, qg, gg, sg,
    pk, pv, pq,
    table, items, kbuf, vbuf, qbuf, gbuf, dq, dk, dv, kout, vout, qout, zero,
    in_sem, out_sem, q_sem, zero_sem,
):
    z, y, c, _ = place()
    scale = 1.0 / math.sqrt(HD)

    def clear(at, carry):
        table[at] = 0
        return carry

    lax.fori_loop(0, NSLOT * 4, clear, 0)
    for yq in range(4):
        def enter(at, carry, yq=yq):
            block = lax.div(at, 3)
            chosen = selected[(((z * 4 + yq) * 2 + c) * BLK_DEV + block) * 3 + lax.rem(at, 3)]
            owner = lax.div(chosen, BLK_DEV)
            here = (chosen > 0) & (lax.rem(lax.div(owner, 2), 4) == y)
            slot = (lax.div(owner, 8) * 2 + lax.rem(owner, 2)) * BLK_DEV + lax.rem(chosen, BLK_DEV)

            @pl.when(here)
            def _():
                table[slot * 4 + yq] = 1 + yq * BLK_DEV + block
            return carry

        lax.fori_loop(0, BLK_DEV * 3, enter, 0)
    for block in range(BLK_DEV):
        later = ((z * 4 + y) * 2 + c) * BLK_DEV + block > 0
        table[FIRST * 4 + block] = jnp.where(later, 1 + y * BLK_DEV + block, 0)

    def compact(at, count):
        entry = table[at]
        items[count] = at * 128 + entry
        return count + jnp.where(entry > 0, 1, 0)

    count = lax.fori_loop(0, NSLOT * 4, compact, 0)
    items[count] = -1

    zero[...] = jnp.zeros_like(zero)

    def idle(slot):
        return (
            table[slot * 4] + table[slot * 4 + 1] + table[slot * 4 + 2] + table[slot * 4 + 3]
        ) == 0

    def blank(slot):
        return [
            pltpu.make_async_copy(zero, ref.at[slot], zero_sem.at[slot, part])
            for part, ref in enumerate((pk, pv))
        ]

    def start_blank(slot, carry):
        @pl.when(idle(slot))
        def _():
            for copy in blank(slot):
                copy.start()
        return carry

    lax.fori_loop(0, NSLOT, start_blank, 0)

    def decode(item):
        slot = lax.div(item, 512)
        entry = lax.rem(item, 128) - 1
        return slot, entry

    def loads(at):
        slot, block = decode(items[at])
        side = lax.rem(at, 2)
        return [
            pltpu.make_async_copy(kg.at[slot], kbuf.at[side], in_sem.at[side, 0]),
            pltpu.make_async_copy(vg.at[slot], vbuf.at[side], in_sem.at[side, 1]),
            pltpu.make_async_copy(qg.at[block], qbuf.at[side], in_sem.at[side, 2]),
            pltpu.make_async_copy(gg.at[block], gbuf.at[side], in_sem.at[side, 3]),
        ]

    @pl.when(count > 0)
    def _():
        for copy in loads(0):
            copy.start()

    dq[...] = jnp.zeros_like(dq)

    def work(side, block):
        for head in range(2):
            part = pl.ds(head * HD, HD)
            k, v = kbuf[side, :, part], vbuf[side, :, part]
            q, g = qbuf[side, :, part], gbuf[side, :, part]
            lse = sg[block, pl.ds(head, 1), :]
            delta = sg[block, pl.ds(2 + head, 1), :]
            p = jnp.exp2(dot(k, q, NT) * (scale * LOG2E) - lse)
            ds = (p * (dot(v, g, NT) - delta)).astype(jnp.bfloat16)
            dv[:, part] += dot(p.astype(jnp.bfloat16), g, NN)
            dk[:, part] += dot(ds, q, NN)
            dq[block, :, part] += dot(ds, k, TN)

    outs = [
        pltpu.make_async_copy(kout, pk.at[0], out_sem.at[0]),
        pltpu.make_async_copy(vout, pv.at[0], out_sem.at[1]),
    ]

    def item_step(at, carry):
        opened, written = carry
        slot, block = decode(items[at])
        following = items[at + 1]
        side = lax.rem(at, 2)

        @pl.when(following >= 0)
        def _():
            for copy in loads(at + 1):
                copy.start()

        for copy in loads(at):
            copy.wait()

        @pl.when(slot != opened)
        def _():
            dk[...] = jnp.zeros_like(dk)
            dv[...] = jnp.zeros_like(dv)

        work(side, block)
        closing = (following < 0) | (lax.div(following, 512) != slot)

        @pl.when(closing)
        def _():
            @pl.when(written > 0)
            def _():
                for copy in outs:
                    copy.wait()
            kout[...] = (dk[...] * scale).astype(jnp.bfloat16)
            vout[...] = dv[...].astype(jnp.bfloat16)
            pltpu.make_async_copy(kout, pk.at[slot], out_sem.at[0]).start()
            pltpu.make_async_copy(vout, pv.at[slot], out_sem.at[1]).start()

        return slot, written + jnp.where(closing, 1, 0)

    lax.fori_loop(0, count, item_step, (-1, 0))

    def finish(block, carry):
        qout[block] = (dq[block] * scale).astype(jnp.bfloat16)
        pltpu.make_async_copy(qout.at[block], pq.at[block], q_sem.at[block]).start()
        return carry

    lax.fori_loop(0, 16, finish, 0)

    @pl.when(count > 0)
    def _():
        for copy in outs:
            copy.wait()

    def drain(block, carry):
        pltpu.make_async_copy(qout.at[block], pq.at[block], q_sem.at[block]).wait()
        return carry

    lax.fori_loop(0, 16, drain, 0)

    def wait_blank(slot, carry):
        @pl.when(idle(slot))
        def _():
            for copy in blank(slot):
                copy.wait()
        return carry

    lax.fori_loop(0, NSLOT, wait_blank, 0)


def scatter_kernel(
    pk, pv, pq, own_q, own_k, own_v,
    out_q, out_k, out_v,
    ownk, ownv, sibk, sibv, relk, relv, fink, finv,
    ownq, relq, finq, accq, acck, accv, fown, frecv, fsum, fsend,
    send, recv, local,
):
    z, y, c, x = place()
    near = neighbours(z, y, c, x)
    greet(list(near.values()))
    started = []

    def remote(index, src, dst, target):
        return pltpu.make_async_remote_copy(
            src_ref=src, dst_ref=dst, send_sem=send.at[index], recv_sem=recv.at[index],
            device_id=target, device_id_type=MESH,
        )

    def go(index, src, dst, target):
        copy = remote(index, src, dst, target)
        copy.start()
        started.append(copy)

    def came(index, dst):
        remote(index, dst, dst, near["sib"]).wait_recv()

    def column(z_at, c_at):
        return pl.ds((z_at * 2 + c_at) * BLK_DEV, BLK_DEV)

    def local_copy(index, src, dst):
        copy = pltpu.make_async_copy(src, dst, local.at[index])
        copy.start()
        return copy

    hops = (2, 1, 3, 0)
    parts = ((pk, ownk, sibk), (pv, ownv, sibv))
    locals_k = []
    for j, hop in enumerate(hops):
        for part, (ref, held, other) in enumerate(parts):
            go(2 * j + part, ref.at[column(after(z, hop), 1 - c)], other.at[j], near["sib"])
            locals_k.append(local_copy(2 * j + part, ref.at[column(after(z, hop), c)], held.at[j]))
        if j == 0:
            for core, (mine, theirs) in enumerate(((pk, pv), (pv, pk))):
                @pl.when(c == core)
                def _(mine=mine, theirs=theirs):
                    remote(20, theirs.at[FIRST], frecv.at[0], near["sib"]).start()
                    pltpu.make_async_copy(mine.at[FIRST], fown, local.at[8]).start()
    locals_q = [
        local_copy(9 + j, pq.at[pl.ds(after(y, hop) * BLK_DEV, BLK_DEV)], ownq.at[j])
        for j, hop in enumerate(hops)
    ]
    locals_own = [
        local_copy(13 + j, src, dst)
        for j, (src, dst) in enumerate(((own_q, accq), (own_k, acck), (own_v, accv)))
    ]

    def add(dst, src, blocks=BLK_DEV):
        def one(block, carry):
            dst[block] = (dst[block].astype(jnp.float32) + src[block].astype(jnp.float32)).astype(
                jnp.bfloat16
            )
            return carry

        lax.fori_loop(0, blocks, one, 0)

    def merge(j, part):
        _, held, other = parts[part]
        locals_k[2 * j + part].wait()
        came(2 * j + part, other.at[j])
        add(held.at[j], other.at[j])

    merge(0, 0)
    go(14, ownk.at[0], relk, near["zr"])
    merge(0, 1)
    go(15, ownv.at[0], relv, near["zl"])

    def f_copy(index, src, dst, target):
        return remote(index, src, dst, target)

    f_sends = [
        ((y == 2) | (y == 1), f_copy(21, fsend.at[0], frecv.at[1], near["yl"])),
        (y == 3, f_copy(22, fsend.at[0], frecv.at[2], near["yr"])),
        ((y == 0) & ((z == 2) | (z == 1)), f_copy(23, fsend.at[1], frecv.at[3], near["zl"])),
        ((y == 0) & (z == 3), f_copy(24, fsend.at[1], frecv.at[4], near["zr"])),
    ]

    def f_take(at):
        came(20 + at, frecv.at[at])
        fsum[...] += frecv[at].astype(jnp.float32)

    def f_send(at):
        condition, copy = f_sends[at]

        @pl.when(condition)
        def _():
            fsend[at // 2] = fsum[...].astype(jnp.bfloat16)
            copy.start()

    pltpu.make_async_copy(pk.at[FIRST], fown, local.at[8]).wait()
    came(20, frecv.at[0])
    fsum[...] = fown[...].astype(jnp.float32) + frecv[0].astype(jnp.float32)

    @pl.when(y == 1)
    def _():
        f_take(1)

    f_send(0)
    f_send(1)

    locals_q[0].wait()
    go(8, ownq.at[0, pl.ds(0, 2)], relq.at[0], near["yr"])
    go(9, ownq.at[0, pl.ds(2, 2)], relq.at[1], near["yl"])
    merge(1, 1)
    go(16, ownv.at[1], finv.at[0], near["zr"])
    merge(2, 0)
    go(17, ownk.at[2], fink.at[1], near["zl"])
    locals_q[1].wait()
    go(10, ownq.at[1, pl.ds(2, 2)], finq.at[0, pl.ds(2, 2)], near["yr"])
    locals_q[2].wait()
    go(11, ownq.at[2, pl.ds(0, 2)], finq.at[1, pl.ds(0, 2)], near["yl"])

    @pl.when(y == 0)
    def _():
        f_take(1)
        f_take(2)

        @pl.when(z == 1)
        def _():
            f_take(3)

    f_send(2)
    f_send(3)

    merge(1, 0)
    merge(2, 1)
    merge(3, 0)
    merge(3, 1)
    came(8, relq.at[0])
    add(ownq.at[1], relq.at[0], 2)
    go(12, ownq.at[1, pl.ds(0, 2)], finq.at[0, pl.ds(0, 2)], near["yr"])
    came(9, relq.at[1])
    add(ownq.at[2, pl.ds(2, 2)], relq.at[1], 2)
    go(13, ownq.at[2, pl.ds(2, 2)], finq.at[1, pl.ds(2, 2)], near["yl"])
    came(14, relk)
    add(ownk.at[1], relk)
    go(18, ownk.at[1], fink.at[0], near["zr"])
    came(15, relv)
    add(ownv.at[2], relv)
    go(19, ownv.at[2], finv.at[1], near["zl"])

    top = (z == 0) & (y == 0)

    @pl.when(top)
    def _():
        f_take(3)
        f_take(4)

    def total(acc, parts_in, out):
        def one(block, carry):
            value = acc[block]
            for ref in parts_in:
                value += ref[block].astype(jnp.float32)
            out[block] = value.astype(jnp.bfloat16)
            return carry

        lax.fori_loop(0, BLK_DEV, one, 0)

    locals_q[3].wait()
    for copy in locals_own:
        copy.wait()

    @pl.when(top & (c == 1))
    def _():
        fsend[1] = fsum[...].astype(jnp.bfloat16)
        remote(25, fsend.at[1], frecv.at[5], near["sib"]).start()

    @pl.when(top & (c == 0))
    def _():
        came(25, frecv.at[5])
        acck[0] += fsum[...]
        accv[0] += frecv[5].astype(jnp.float32)

    came(10, finq.at[0, pl.ds(2, 2)])
    came(11, finq.at[1, pl.ds(0, 2)])
    came(12, finq.at[0, pl.ds(0, 2)])
    came(13, finq.at[1, pl.ds(2, 2)])
    total(accq, (ownq.at[3], finq.at[0], finq.at[1]), out_q)
    came(17, fink.at[1])
    came(16, finv.at[0])
    came(18, fink.at[0])
    total(acck, (ownk.at[3], fink.at[0], fink.at[1]), out_k)
    came(19, finv.at[1])
    total(accv, (ownv.at[3], finv.at[0], finv.at[1]), out_v)

    for copy in started:
        copy.wait_send()
    remote(20, fown, frecv.at[0], near["sib"]).wait_send()
    for condition, copy in f_sends + [
        (top & (c == 1), remote(25, fsend.at[1], frecv.at[5], near["sib"]))
    ]:
        @pl.when(condition)
        def _(copy=copy):
            copy.wait_send()


def body(query, keys, values, output, d_out, row_logsum, selected):
    bf16, f32 = jnp.bfloat16, jnp.float32
    any_spec = pl.BlockSpec(memory_space=pl.ANY)
    vmem_spec = pl.BlockSpec(memory_space=pltpu.VMEM)
    smem_spec = pl.BlockSpec(memory_space=pltpu.SMEM)
    blocked = (BLK_DEV, BLOCK, WIDTH)
    shape = jax.ShapeDtypeStruct
    dma, vmem, smem = pltpu.SemaphoreType.DMA, pltpu.VMEM, pltpu.SMEM
    kg, vg, qg, gg, sg, own_q, own_k, own_v = pl.pallas_call(
        gather_kernel,
        out_shape=[
            shape((NSLOT, BLOCK, WIDTH), bf16),
            shape((NSLOT, BLOCK, WIDTH), bf16),
            shape((16, BLOCK, WIDTH), bf16),
            shape((16, BLOCK, WIDTH), bf16),
            shape((16, 8, BLOCK), f32),
            shape(blocked, f32),
            shape(blocked, f32),
            shape(blocked, f32),
        ],
        in_specs=[any_spec] * 5 + [vmem_spec],
        out_specs=[any_spec] * 8,
        scratch_shapes=[
            vmem(blocked, bf16),
            vmem(blocked, bf16),
            vmem(blocked, bf16),
            vmem(blocked, bf16),
            vmem(blocked, bf16),
            vmem((BLK_DEV, 8, BLOCK), f32),
            vmem(blocked, f32),
            vmem(blocked, f32),
            vmem(blocked, f32),
            dma((34,)),
            dma((28,)),
            dma((15,)),
        ],
        compiler_params=pltpu.CompilerParams(
            collective_id=0, has_side_effects=True, vmem_limit_bytes=VMEM
        ),
        name="gather",
    )(
        keys.reshape(blocked), values.reshape(blocked), query.reshape(blocked),
        d_out, output.reshape(blocked), row_logsum,
    )
    pk, pv, pq = pl.pallas_call(
        pair_kernel,
        out_shape=[
            shape((NSLOT, BLOCK, WIDTH), bf16),
            shape((NSLOT, BLOCK, WIDTH), bf16),
            shape((16, BLOCK, WIDTH), bf16),
        ],
        in_specs=[smem_spec] + [any_spec] * 4 + [vmem_spec],
        out_specs=[any_spec] * 3,
        scratch_shapes=[
            smem((NSLOT * 4,), jnp.int32),
            smem((NSLOT * 4 + 1,), jnp.int32),
            vmem((2, BLOCK, WIDTH), bf16),
            vmem((2, BLOCK, WIDTH), bf16),
            vmem((2, BLOCK, WIDTH), bf16),
            vmem((2, BLOCK, WIDTH), bf16),
            vmem((16, BLOCK, WIDTH), f32),
            vmem((BLOCK, WIDTH), f32),
            vmem((BLOCK, WIDTH), f32),
            vmem((BLOCK, WIDTH), bf16),
            vmem((BLOCK, WIDTH), bf16),
            vmem((16, BLOCK, WIDTH), bf16),
            vmem((BLOCK, WIDTH), bf16),
            dma((2, 4)),
            dma((2,)),
            dma((16,)),
            dma((NSLOT, 2)),
        ],
        compiler_params=pltpu.CompilerParams(vmem_limit_bytes=VMEM),
        name="pairs",
    )(selected.reshape(-1), kg, vg, qg, gg, sg)
    out_q, out_k, out_v = pl.pallas_call(
        scatter_kernel,
        out_shape=[shape(blocked, bf16)] * 3,
        in_specs=[any_spec] * 6,
        out_specs=[vmem_spec] * 3,
        scratch_shapes=[
            vmem((4,) + blocked, bf16),
            vmem((4,) + blocked, bf16),
            vmem((4,) + blocked, bf16),
            vmem((4,) + blocked, bf16),
            vmem(blocked, bf16),
            vmem(blocked, bf16),
            vmem((2,) + blocked, bf16),
            vmem((2,) + blocked, bf16),
            vmem((4,) + blocked, bf16),
            vmem((2, 2, BLOCK, WIDTH), bf16),
            vmem((2,) + blocked, bf16),
            vmem(blocked, f32),
            vmem(blocked, f32),
            vmem(blocked, f32),
            vmem((BLOCK, WIDTH), bf16),
            vmem((6, BLOCK, WIDTH), bf16),
            vmem((BLOCK, WIDTH), f32),
            vmem((2, BLOCK, WIDTH), bf16),
            dma((26,)),
            dma((26,)),
            dma((16,)),
        ],
        compiler_params=pltpu.CompilerParams(
            collective_id=1, has_side_effects=True, vmem_limit_bytes=VMEM
        ),
        name="scatter",
    )(pk, pv, pq, own_q, own_k, own_v)
    flat = (BLK_DEV * BLOCK, WIDTH)
    return out_q.reshape(flat), out_k.reshape(flat), out_v.reshape(flat)


def solution(mesh):
    in_specs = (
        P("seq", "head"),
        P("seq", "head"),
        P("seq", "head"),
        P("seq", "head"),
        P(("seq", "head"), None),
        P("head", "seq"),
        P(),
    )
    out_specs = (P("seq", "head"), P("seq", "head"), P("seq", "head"))
    return jax.shard_map(body, mesh=mesh, in_specs=in_specs, out_specs=out_specs, check_vma=False)
```

time: 283 us -> 252 us (0.89)
  local copies, waits for them, and re-layouts: 24 us -> 7.16 us
  Pallas kernels: 257 us -> 244 us
    pallas_call x1, Pallas kernels: 146 us -> 100 us  [body(): pl.pallas_call(scatter_kernel, out_shape=[shape(blocked, bf16)] * 3, in_s...]
    pallas_call x1, Pallas kernels: 80.9 us -> 119 us  [body(): pl.pallas_call(gather_kernel, out_shape=[shape((NSLOT, BLOCK, WIDTH), bf1...]
    unnamed x24 -> x6, local copies, waits for them, and re-layouts: 23.8 us -> 6.37 us
    pallas_call x1, Pallas kernels: 30.5 us -> 25 us  [body(): pl.pallas_call(pair_kernel, out_shape=[shape((NSLOT, BLOCK, WIDTH), bf16)...]
where the time goes in v2:
time: 252 us
  Pallas kernels  244 us (97%)
  local copies, waits for them, and re-layouts  7.16 us (3%)
    pallas_call x1, Pallas kernels, body(): pl.pallas_call(gather_kernel, out_shape=[shape((NSLOT, BLOCK, WIDTH), bf1...  119 us
    pallas_call x1, Pallas kernels, body(): pl.pallas_call(scatter_kernel, out_shape=[shape(blocked, bf16)] * 3, in_s...  100 us
    pallas_call x1, Pallas kernels, body(): pl.pallas_call(pair_kernel, out_shape=[shape((NSLOT, BLOCK, WIDTH), bf16)...  25 us
    unnamed x6, local copies, waits for them, and re-layouts  6.37 us

profile of v2, /device:TPU:0, one launch (start us, length us, event | category | flops | bytes accessed | tf_op | source)
XLA Modules:
  0.0 251.8 jit_solution(11612283405868075184)
XLA Ops:
  0.6 0.8 copy.10
  1.4 0.8 reshape.30.selected
  2.2 119.0 %gather.1 = (bf16[33,512,256]{2,1,0:T(8,128)(2,1)}, bf16[33,512,256]{2,1,0:T(8,128)(2,1)}, bf16[16,512,256]{2,1,0:T(8,128)(2,1)}, bf16[16,512,256]{2,1,0:T(8,128...) custom-call(bf16[4,512,256]{2,1,0:T(8,128)(2,1)} %bitcast.7, ...), custom_call_target="tpu_custom_call" | custom-call | tf_op jit(solution)/shard_map/gather/pallas_call | solution.py:670
  121.2 25.0 %pairs.1 = (bf16[33,512,256]{2,1,0:T(8,128)(2,1)}, bf16[33,512,256]{2,1,0:T(8,128)(2,1)}, bf16[16,512,256]{2,1,0:T(8,128)(2,1)}) custom-call(s32[384]{0:T(512)} %reshape.30.selected, bf16[33,512,256]{2,1,0:T(8,128)(2,1)} %get-tuple-element.17.kg, bf16[33,512,256]{2,1,0:T(8,128)(2,1)} %get-tuple-element.18.vg, bf16[16,512,256]{2,1,0:T(8,128)(2,1)} %get-tuple-element.19.qg, ...), custom_call_target="tpu_custom_call" | custom-call | tf_op jit(solution)/shard_map/pairs/pallas_call | solution.py:706
  146.2 100.0 %scatter.1 = (bf16[4,512,256]{2,1,0:T(8,128)(2,1)}, bf16[4,512,256]{2,1,0:T(8,128)(2,1)}, bf16[4,512,256]{2,1,0:T(8,128)(2,1)}) custom-call(bf16[33,512,256]{2,1,0:T(8,128)(2,1)} %get-tuple-element.22.pk, bf16[33,512,256]{2,1,0:T(8,128)(2,1)} %get-tuple-element.23.pv, bf16[16,512,256]{2,1,0:T(8,128)(2,1)} %get-tuple-element.24.pq, ...), custom_call_target="tpu_custom_call" | custom-call | tf_op jit(solution)/shard_map/scatter/pallas_call | solution.py:737
  246.2 0.0 copy-start
  246.2 2.4 copy.14
  248.6 2.3 copy.15
  250.8 0.0 copy-done
  250.8 1.0 copy.16
Async XLA Ops:
  246.2 4.6 %copy-start = (bf16[4,512,256]{2,1,0:T(8,128)(2,1)S(1)}, bf16[4,512,256]{2,1,0:T(8,128)(2,1)}, u32[]{:S(2)}) copy-start(bf16[4,512,256]{2,1,0:T(8,128)(2,1)} %get-tuple-element.30) | copy-start | bytes 3145732

commit v3 on v2

--- a/solution.py
+++ b/solution.py
@@ -14,8 +14,7 @@
 WIDTH = 256
 BLK_DEV = 4
 RING = 4
-NSLOT = 33
-FIRST = 32
+NSLOT = 32
 LOG2E = math.log2(math.e)
 VMEM = 60 * 1024 * 1024
 
@@ -61,8 +60,8 @@
 
 def gather_kernel(
     keys, values, query, d_out, output, logsum,
-    kg, vg, qg, gg, sg, own_q, own_k, own_v,
-    grad, outv, kv, vv, qv, stats, accq, acck, accv, send, recv, local,
+    kg, vg, qg, gg, sg, own_q, own_k, own_v, own_f,
+    grad, outv, kv, vv, qv, stats, accq, acck, accv, fblk, accf, fout, send, recv, local,
 ):
     z, y, c, x = place()
     near = neighbours(z, y, c, x)
@@ -70,23 +69,42 @@
     greet(list(near.values()) + others)
     started = []
 
-    def remote(index, src, dst, target):
+    def remote(index, src, dst, target, chunk=0):
         return pltpu.make_async_remote_copy(
-            src_ref=src, dst_ref=dst, send_sem=send.at[index], recv_sem=recv.at[index],
+            src_ref=src, dst_ref=dst,
+            send_sem=send.at[index, chunk], recv_sem=recv.at[index, chunk],
             device_id=target, device_id_type=MESH,
         )
 
-    def go(index, src, dst, target):
-        copy = remote(index, src, dst, target)
+    def go(index, src, dst, target, chunk=0):
+        copy = remote(index, src, dst, target, chunk)
         copy.start()
         started.append(copy)
-        return copy
+
+    def spread(index, src, dst, piece, target):
+        for chunk in range(BLK_DEV):
+            go(index, src.at[chunk], dst.at[piece + chunk], target, chunk)
+
+    def arrived(index, ref, piece):
+        for chunk in range(BLK_DEV):
+            at = ref.at[piece + chunk]
+            remote(index, at, at, near["sib"], chunk).wait_recv()
+
+    def relay(came, ref, piece, *onward):
+        for chunk in range(BLK_DEV):
+            at = ref.at[piece + chunk]
+            remote(came, at, at, near["sib"], chunk).wait_recv()
+            for index, target in onward:
+                go(index, at, at, target, chunk)
 
     def column(z_at, c_at):
-        return pl.ds((z_at * 2 + c_at) * BLK_DEV, BLK_DEV)
+        return (z_at * 2 + c_at) * BLK_DEV
 
     def row(y_at):
-        return pl.ds(y_at * BLK_DEV, BLK_DEV)
+        return y_at * BLK_DEV
+
+    def four(start):
+        return pl.ds(start, BLK_DEV)
 
     zl, zr, zo = after(z, 3), after(z, 1), after(z, 2)
     yl, yr = after(y, 3), after(y, 1)
@@ -94,34 +112,37 @@
     root = top & (c == 0)
 
     first_own = [
-        pltpu.make_async_copy(keys.at[0], kg.at[FIRST], local.at[0]),
-        pltpu.make_async_copy(values.at[0], vg.at[FIRST], local.at[1]),
+        pltpu.make_async_copy(keys.at[0], fblk.at[0], local.at[0]),
+        pltpu.make_async_copy(values.at[0], fblk.at[1], local.at[1]),
     ]
 
-    def first_copy(ref, send_at, recv_at, target):
+    def first_copy(part, send_at, recv_at, target):
         return pltpu.make_async_remote_copy(
-            src_ref=ref.at[FIRST], dst_ref=ref.at[FIRST],
-            send_sem=send.at[send_at], recv_sem=recv.at[recv_at],
+            src_ref=fblk.at[part], dst_ref=fblk.at[part],
+            send_sem=send.at[send_at, 0], recv_sem=recv.at[recv_at, 0],
             device_id=target, device_id_type=MESH,
         )
 
-    first_sends = []
-    for core, ref in enumerate((kg, vg)):
-        mine = c == core
-        first_sends += [
-            (mine & (z == 0) & (y <= 1), first_copy(ref, 28, 26, near["yr"])),
-            (mine & (z == 0) & (y == 0), first_copy(ref, 29, 26, near["yl"])),
-            (mine & (z <= 1), first_copy(ref, 30, 26, near["zr"])),
-            (mine & (z == 0), first_copy(ref, 31, 26, near["zl"])),
-            (mine & jnp.logical_not(top & (c == 1)), first_copy(ref, 32, 27, near["sib"])),
-        ]
-    first_start = first_copy(vg, 33, 26, near["sib"])
+    first_sends = [
+        ((z == 0) & (y <= 1), first_copy(c, 28, 26, near["yr"])),
+        ((z == 0) & (y == 0), first_copy(c, 29, 26, near["yl"])),
+        (z <= 1, first_copy(c, 30, 26, near["zr"])),
+        (z == 0, first_copy(c, 31, 26, near["zl"])),
+        (jnp.logical_not(top & (c == 1)), first_copy(c, 32, 27, near["sib"])),
+    ]
+    first_start = first_copy(1, 33, 26, near["sib"])
 
     def send_first():
         for condition, copy in first_sends:
             @pl.when(condition)
             def _(copy=copy):
                 copy.start()
+
+    def pass_first(condition):
+        @pl.when(condition)
+        def _():
+            first_copy(c, 28, 26, near["sib"]).wait_recv()
+            send_first()
 
     @pl.when(root)
     def _():
@@ -132,10 +153,7 @@
         first_start.start()
         send_first()
 
-    @pl.when(top & (c == 1))
-    def _():
-        first_start.wait_recv()
-        send_first()
+    pass_first(top & (c == 1))
 
     for step in (1, 2, 3):
         to = after(x, step)
@@ -154,32 +172,30 @@
         pltpu.make_async_copy(values, vv, local.at[5]),
         pltpu.make_async_copy(query, qv, local.at[6]),
     ]
-    kept = [
-        pltpu.make_async_copy(keys, kg.at[column(z, c)], local.at[7]),
-        pltpu.make_async_copy(values, vg.at[column(z, c)], local.at[8]),
-        pltpu.make_async_copy(query, qg.at[row(y)], local.at[9]),
-    ]
-    for copy in to_vmem + kept:
+    kept = []
+    for copy in to_vmem:
         copy.start()
 
     own = column(z, c)
-    go(0, keys, kg.at[own], near["zr"])
-    go(1, values, vg.at[own], near["zl"])
-    go(14, query, qg.at[row(y)], near["yr"])
-    go(15, query, qg.at[row(y)], near["yl"])
-    go(4, keys, kg.at[own], near["sib"])
-    go(5, values, vg.at[own], near["sib"])
-
+    spread(0, keys, kg, own, near["zr"])
+    spread(1, values, vg, own, near["zl"])
+    spread(14, query, qg, row(y), near["yr"])
+    spread(15, query, qg, row(y), near["yl"])
+    spread(2, values, vg, own, near["zr"])
+    spread(3, keys, kg, own, near["zl"])
+    spread(4, keys, kg, own, near["sib"])
+    spread(5, values, vg, own, near["sib"])
+
+    pass_first((z == 0) & ((y == 1) | (y == 3)))
     to_vmem[0].wait()
     to_vmem[1].wait()
     for step in (1, 2, 3):
         remote(22 + step, grad.at[x], grad.at[x], others[step - 1]).wait_recv()
-    go(16, grad, gg.at[row(y)], near["yl"])
-    go(17, grad, gg.at[row(y)], near["yr"])
-    go(2, values, vg.at[own], near["zr"])
-    go(3, keys, kg.at[own], near["zl"])
-    kept.append(pltpu.make_async_copy(grad, gg.at[row(y)], local.at[10]))
+    spread(16, grad, gg, row(y), near["yl"])
+    spread(17, grad, gg, row(y), near["yr"])
+    kept.append(pltpu.make_async_copy(grad, gg.at[four(row(y))], local.at[10]))
     kept[-1].start()
+    pass_first((z == 0) & (y == 2))
     stats[...] = jnp.zeros_like(stats)
 
     ones = jnp.ones((8, HD), jnp.bfloat16)
@@ -194,18 +210,18 @@
             stats[block, pl.ds(head, 1), :] = (
                 logsum[pl.ds(head, 1), pl.ds(block * BLOCK, BLOCK)] * LOG2E
             )
-    go(18, stats, sg.at[row(y)], near["yr"])
-    go(19, stats, sg.at[row(y)], near["yl"])
-    kept.append(pltpu.make_async_copy(stats, sg.at[row(y)], local.at[11]))
+    go(18, stats, sg.at[four(row(y))], near["yr"])
+    go(19, stats, sg.at[four(row(y))], near["yl"])
+    kept.append(pltpu.make_async_copy(stats, sg.at[four(row(y))], local.at[11]))
     kept[-1].start()
-
-    @pl.when(jnp.logical_not(top))
-    def _():
-        first_copy(kg, 28, 26, near["sib"]).wait_recv()
-        send_first()
 
     for copy in to_vmem[2:]:
         copy.wait()
+    for index, (src, dst) in enumerate(
+        ((kv, kg.at[four(own)]), (vv, vg.at[four(own)]), (qv, qg.at[four(row(y))]))
+    ):
+        kept.append(pltpu.make_async_copy(src, dst, local.at[7 + index]))
+        kept[-1].start()
     scale = 1.0 / math.sqrt(HD)
 
     def own_block(block, carry):
@@ -224,54 +240,60 @@
             accq[block, :, part] = dot(ds, k, TN) * scale
         return carry
 
+    def first_block(block, carry):
+        for head in range(2):
+            part = pl.ds(head * HD, HD)
+            k, v, q, g = fblk[0, :, part], fblk[1, :, part], qv[block, :, part], grad[block, :, part]
+            lse = stats[block, pl.ds(head, 1), :]
+            delta = stats[block, pl.ds(2 + head, 1), :]
+            p = jnp.exp2(dot(k, q, NT) * (scale * LOG2E) - lse)
+            ds = (p * (dot(v, g, NT) - delta)).astype(jnp.bfloat16)
+            accf[1, :, part] += dot(p.astype(jnp.bfloat16), g, NN)
+            accf[0, :, part] += dot(ds, q, NN) * scale
+            accq[block, :, part] += dot(ds, k, TN) * scale
+        return carry
+
     lax.fori_loop(0, BLK_DEV, own_block, 0)
-    for index, (src, dst) in enumerate(((accq, own_q), (acck, own_k), (accv, own_v))):
+    for index, (src, dst) in enumerate(((acck, own_k), (accv, own_v))):
         kept.append(pltpu.make_async_copy(src, dst, local.at[12 + index]))
         kept[-1].start()
-
-    def arrived(index, ref, piece, source):
-        remote(index, ref.at[piece], ref.at[piece], source).wait_recv()
-
-    def forward(index, ref, piece, target):
-        go(index, ref.at[piece], ref.at[piece], target)
+    pass_first((z == 1) | (z == 3))
 
     left_k, right_k, far_k = column(zl, c), column(zr, c), column(zo, c)
-    arrived(0, kg, left_k, near["zl"])
-    forward(6, kg, left_k, near["zr"])
-    arrived(1, vg, right_k, near["zr"])
-    forward(7, vg, right_k, near["zl"])
-    arrived(14, qg, row(yl), near["yl"])
-    forward(20, qg, row(yl), near["yr"])
-    arrived(18, sg, row(yl), near["yl"])
-    forward(22, sg, row(yl), near["yr"])
-    arrived(16, gg, row(yr), near["yr"])
-    forward(21, gg, row(yr), near["yl"])
-    forward(8, kg, left_k, near["sib"])
-    forward(9, vg, right_k, near["sib"])
-    arrived(2, vg, left_k, near["zl"])
-    forward(10, vg, left_k, near["sib"])
-    arrived(3, kg, right_k, near["zr"])
-    forward(11, kg, right_k, near["sib"])
-    arrived(6, kg, far_k, near["zl"])
-    forward(12, kg, far_k, near["sib"])
-    arrived(7, vg, far_k, near["zr"])
-    forward(13, vg, far_k, near["sib"])
-    arrived(15, qg, row(yr), near["yr"])
-    arrived(17, gg, row(yl), near["yl"])
-    arrived(19, sg, row(yr), near["yr"])
-    arrived(20, qg, row(after(y, 2)), near["yl"])
-    arrived(21, gg, row(after(y, 2)), near["yr"])
-    arrived(22, sg, row(after(y, 2)), near["yl"])
+    relay(0, kg, left_k, (6, near["zr"]), (8, near["sib"]))
+    relay(1, vg, right_k, (7, near["zl"]), (9, near["sib"]))
+    relay(14, qg, row(yl), (20, near["yr"]))
+    stats_in = [sg.at[four(row(after(y, step)))] for step in (3, 1, 2)]
+    remote(18, stats_in[0], stats_in[0], near["yl"]).wait_recv()
+    go(22, stats_in[0], stats_in[0], near["yr"])
+    relay(16, gg, row(yr), (21, near["yl"]))
+    pass_first(z == 2)
 
     @pl.when(jnp.logical_not(root))
     def _():
-        first_copy(kg, 32, 27, near["sib"]).wait_recv()
-
+        first_copy(1 - c, 32, 27, near["sib"]).wait_recv()
+
+    accf[...] = jnp.zeros_like(accf)
+    lax.fori_loop(jnp.where(root, 1, 0), BLK_DEV, first_block, 0)
+    fout[...] = accf[...].astype(jnp.bfloat16)
+    for index, (src, dst) in enumerate(((accq, own_q), (fout, own_f))):
+        kept.append(pltpu.make_async_copy(src, dst, local.at[14 + index]))
+        kept[-1].start()
+    relay(2, vg, left_k, (10, near["sib"]))
+    relay(3, kg, right_k, (11, near["sib"]))
+    relay(6, kg, far_k, (12, near["sib"]))
+    relay(7, vg, far_k, (13, near["sib"]))
+    arrived(15, qg, row(yr))
+    arrived(17, gg, row(yl))
+    arrived(20, qg, row(after(y, 2)))
+    arrived(21, gg, row(after(y, 2)))
+    remote(19, stats_in[1], stats_in[1], near["yr"]).wait_recv()
+    remote(22, stats_in[2], stats_in[2], near["yl"]).wait_recv()
     for index, ref, z_at in (
         (4, kg, z), (5, vg, z), (8, kg, zl), (9, vg, zr),
         (10, vg, zl), (11, kg, zr), (12, kg, zo), (13, vg, zo),
     ):
-        arrived(index, ref, column(z_at, 1 - c), near["sib"])
+        arrived(index, ref, column(z_at, 1 - c))
     for copy in kept:
         copy.wait()
     for copy in started:
@@ -296,35 +318,21 @@
     z, y, c, _ = place()
     scale = 1.0 / math.sqrt(HD)
 
-    def clear(at, carry):
+    for at in range(NSLOT * 4):
         table[at] = 0
-        return carry
-
-    lax.fori_loop(0, NSLOT * 4, clear, 0)
     for yq in range(4):
-        def enter(at, carry, yq=yq):
-            block = lax.div(at, 3)
-            chosen = selected[(((z * 4 + yq) * 2 + c) * BLK_DEV + block) * 3 + lax.rem(at, 3)]
+        for at in range(BLK_DEV * 3):
+            block = at // 3
+            chosen = selected[(((z * 4 + yq) * 2 + c) * BLK_DEV + block) * 3 + at % 3]
             owner = lax.div(chosen, BLK_DEV)
             here = (chosen > 0) & (lax.rem(lax.div(owner, 2), 4) == y)
             slot = (lax.div(owner, 8) * 2 + lax.rem(owner, 2)) * BLK_DEV + lax.rem(chosen, BLK_DEV)
-
-            @pl.when(here)
-            def _():
-                table[slot * 4 + yq] = 1 + yq * BLK_DEV + block
-            return carry
-
-        lax.fori_loop(0, BLK_DEV * 3, enter, 0)
-    for block in range(BLK_DEV):
-        later = ((z * 4 + y) * 2 + c) * BLK_DEV + block > 0
-        table[FIRST * 4 + block] = jnp.where(later, 1 + y * BLK_DEV + block, 0)
-
-    def compact(at, count):
+            table[jnp.where(here, slot * 4 + yq, NSLOT * 4)] = 1 + yq * BLK_DEV + block
+    count = 0
+    for at in range(NSLOT * 4):
         entry = table[at]
         items[count] = at * 128 + entry
-        return count + jnp.where(entry > 0, 1, 0)
-
-    count = lax.fori_loop(0, NSLOT * 4, compact, 0)
+        count = count + jnp.where(entry > 0, 1, 0)
     items[count] = -1
 
     zero[...] = jnp.zeros_like(zero)
@@ -455,7 +463,7 @@
 
 
 def scatter_kernel(
-    pk, pv, pq, own_q, own_k, own_v,
+    pk, pv, pq, own_q, own_k, own_v, own_f,
     out_q, out_k, out_v,
     ownk, ownv, sibk, sibv, relk, relv, fink, finv,
     ownq, relq, finq, accq, acck, accv, fown, frecv, fsum, fsend,
@@ -496,11 +504,8 @@
             go(2 * j + part, ref.at[column(after(z, hop), 1 - c)], other.at[j], near["sib"])
             locals_k.append(local_copy(2 * j + part, ref.at[column(after(z, hop), c)], held.at[j]))
         if j == 0:
-            for core, (mine, theirs) in enumerate(((pk, pv), (pv, pk))):
-                @pl.when(c == core)
-                def _(mine=mine, theirs=theirs):
-                    remote(20, theirs.at[FIRST], frecv.at[0], near["sib"]).start()
-                    pltpu.make_async_copy(mine.at[FIRST], fown, local.at[8]).start()
+            remote(20, own_f.at[1 - c], frecv.at[0], near["sib"]).start()
+            mine_f = local_copy(8, own_f.at[c], fown)
     locals_q = [
         local_copy(9 + j, pq.at[pl.ds(after(y, hop) * BLK_DEV, BLK_DEV)], ownq.at[j])
         for j, hop in enumerate(hops)
@@ -552,7 +557,7 @@
             fsend[at // 2] = fsum[...].astype(jnp.bfloat16)
             copy.start()
 
-    pltpu.make_async_copy(pk.at[FIRST], fown, local.at[8]).wait()
+    mine_f.wait()
     came(20, frecv.at[0])
     fsum[...] = fown[...].astype(jnp.float32) + frecv[0].astype(jnp.float32)
 
@@ -667,7 +672,7 @@
     blocked = (BLK_DEV, BLOCK, WIDTH)
     shape = jax.ShapeDtypeStruct
     dma, vmem, smem = pltpu.SemaphoreType.DMA, pltpu.VMEM, pltpu.SMEM
-    kg, vg, qg, gg, sg, own_q, own_k, own_v = pl.pallas_call(
+    kg, vg, qg, gg, sg, own_q, own_k, own_v, own_f = pl.pallas_call(
         gather_kernel,
         out_shape=[
             shape((NSLOT, BLOCK, WIDTH), bf16),
@@ -678,9 +683,10 @@
             shape(blocked, f32),
             shape(blocked, f32),
             shape(blocked, f32),
+            shape((2, BLOCK, WIDTH), bf16),
         ],
         in_specs=[any_spec] * 5 + [vmem_spec],
-        out_specs=[any_spec] * 8,
+        out_specs=[any_spec] * 9,
         scratch_shapes=[
             vmem(blocked, bf16),
             vmem(blocked, bf16),
@@ -691,9 +697,12 @@
             vmem(blocked, f32),
             vmem(blocked, f32),
             vmem(blocked, f32),
-            dma((34,)),
-            dma((28,)),
-            dma((15,)),
+            vmem((2, BLOCK, WIDTH), bf16),
+            vmem((2, BLOCK, WIDTH), f32),
+            vmem((2, BLOCK, WIDTH), bf16),
+            dma((34, BLK_DEV)),
+            dma((28, BLK_DEV)),
+            dma((16,)),
         ],
         compiler_params=pltpu.CompilerParams(
             collective_id=0, has_side_effects=True, vmem_limit_bytes=VMEM
@@ -713,7 +722,7 @@
         in_specs=[smem_spec] + [any_spec] * 4 + [vmem_spec],
         out_specs=[any_spec] * 3,
         scratch_shapes=[
-            smem((NSLOT * 4,), jnp.int32),
+            smem((NSLOT * 4 + 1,), jnp.int32),
             smem((NSLOT * 4 + 1,), jnp.int32),
             vmem((2, BLOCK, WIDTH), bf16),
             vmem((2, BLOCK, WIDTH), bf16),
@@ -737,7 +746,7 @@
     out_q, out_k, out_v = pl.pallas_call(
         scatter_kernel,
         out_shape=[shape(blocked, bf16)] * 3,
-        in_specs=[any_spec] * 6,
+        in_specs=[any_spec] * 7,
         out_specs=[vmem_spec] * 3,
         scratch_shapes=[
             vmem((4,) + blocked, bf16),
@@ -766,7 +775,7 @@
             collective_id=1, has_side_effects=True, vmem_limit_bytes=VMEM
         ),
         name="scatter",
-    )(pk, pv, pq, own_q, own_k, own_v)
+    )(pk, pv, pq, own_q, own_k, own_v, own_f)
     flat = (BLK_DEV * BLOCK, WIDTH)
     return out_q.reshape(flat), out_k.reshape(flat), out_v.reshape(flat)
 

time: 252 us -> 225 us (0.89)
  Pallas kernels: 244 us -> 217 us
    pallas_call x1, Pallas kernels: 119 us -> 86.5 us  [body(): pl.pallas_call(gather_kernel, out_shape=[shape((NSLOT, BLOCK, WIDTH), bf1...]
    pallas_call x1, Pallas kernels: 100 us -> 113 us  [body(): pl.pallas_call(scatter_kernel, out_shape=[shape(blocked, bf16)] * 3, in_s...]
    pallas_call x1, Pallas kernels: 25 us -> 17.7 us  [body(): pl.pallas_call(pair_kernel, out_shape=[shape((NSLOT, BLOCK, WIDTH), bf16)...]
where the time goes in v3:
time: 225 us
  Pallas kernels  217 us (96%)
  local copies, waits for them, and re-layouts  7.16 us (3%)
    pallas_call x1, Pallas kernels, body(): pl.pallas_call(scatter_kernel, out_shape=[shape(blocked, bf16)] * 3, in_s...  113 us
    pallas_call x1, Pallas kernels, body(): pl.pallas_call(gather_kernel, out_shape=[shape((NSLOT, BLOCK, WIDTH), bf1...  86.5 us
    pallas_call x1, Pallas kernels, body(): pl.pallas_call(pair_kernel, out_shape=[shape((NSLOT, BLOCK, WIDTH), bf16)...  17.7 us
    unnamed x6, local copies, waits for them, and re-layouts  6.37 us

profile of v3, /device:TPU:0, one launch (start us, length us, event | category | flops | bytes accessed | tf_op | source)
XLA Modules:
  0.0 225.0 jit_solution(12229910210162456565)
XLA Ops:
  0.6 0.8 copy.10
  1.4 0.8 reshape.30.selected
  2.2 86.5 %gather.1 = (bf16[32,512,256]{2,1,0:T(8,128)(2,1)}, bf16[32,512,256]{2,1,0:T(8,128)(2,1)}, bf16[16,512,256]{2,1,0:T(8,128)(2,1)}, bf16[16,512,256]{2,1,0:T(8,128...) custom-call(bf16[4,512,256]{2,1,0:T(8,128)(2,1)} %bitcast.7, ...), custom_call_target="tpu_custom_call" | custom-call | tf_op jit(solution)/shard_map/gather/pallas_call | solution.py:675
  88.7 17.7 %pairs.1 = (bf16[32,512,256]{2,1,0:T(8,128)(2,1)}, bf16[32,512,256]{2,1,0:T(8,128)(2,1)}, bf16[16,512,256]{2,1,0:T(8,128)(2,1)}) custom-call(s32[384]{0:T(512)} %reshape.30.selected, bf16[32,512,256]{2,1,0:T(8,128)(2,1)} %get-tuple-element.18.kg, bf16[32,512,256]{2,1,0:T(8,128)(2,1)} %get-tuple-element.19.vg, bf16[16,512,256]{2,1,0:T(8,128)(2,1)} %get-tuple-element.20.qg, ...), custom_call_target="tpu_custom_call" | custom-call | tf_op jit(solution)/shard_map/pairs/pallas_call | solution.py:715
  106.4 113.0 %scatter.1 = (bf16[4,512,256]{2,1,0:T(8,128)(2,1)}, bf16[4,512,256]{2,1,0:T(8,128)(2,1)}, bf16[4,512,256]{2,1,0:T(8,128)(2,1)}) custom-call(bf16[32,512,256]{2,1,0:T(8,128)(2,1)} %get-tuple-element.23.pk, bf16[32,512,256]{2,1,0:T(8,128)(2,1)} %get-tuple-element.24.pv, bf16[16,512,256]{2,1,0:T(8,128)(2,1)} %get-tuple-element.25.pq, ...), custom_call_target="tpu_custom_call" | custom-call | tf_op jit(solution)/shard_map/scatter/pallas_call | solution.py:746
  219.4 0.0 copy-start
  219.4 2.4 %copy.14 = bf16[2048,256]{1,0:T(8,128)(2,1)} copy(bf16[2048,256]{1,0:T(8,128)(2,1)} %bitcast.13) | data formatting | bytes 2097152
  221.8 2.3 %copy.15 = bf16[2048,256]{1,0:T(8,128)(2,1)} copy(bf16[2048,256]{1,0:T(8,128)(2,1)} %bitcast.12) | data formatting | bytes 2097152
  224.0 0.0 copy-done
  224.0 1.0 copy.16
Async XLA Ops:
  219.4 4.6 %copy-start = (bf16[4,512,256]{2,1,0:T(8,128)(2,1)S(1)}, bf16[4,512,256]{2,1,0:T(8,128)(2,1)}, u32[]{:S(2)}) copy-start(bf16[4,512,256]{2,1,0:T(8,128)(2,1)} %get-tuple-element.32) | copy-start | bytes 3145732

commit v4 on v3

v4 whole, which is shorter than its diff:
```python
import functools
import math

import jax
import jax.numpy as jnp
from jax import lax
from jax.experimental import pallas as pl
from jax.experimental.pallas import tpu as pltpu
from jax.sharding import PartitionSpec as P

MESH = pl.DeviceIdType.MESH
BLOCK = 512
HD = 128
WIDTH = 256
BLK_DEV = 4
RING = 4
NSLOT = 32
LOG2E = math.log2(math.e)
VMEM = 60 * 1024 * 1024


def place():
    seq = lax.axis_index("seq")
    return lax.div(seq, 8), lax.rem(lax.div(seq, 2), 4), lax.rem(seq, 2), lax.axis_index("head")


def device(z, y, c, x):
    return ((z * 4 + y) * 2 + c, x)


def after(index, step):
    return lax.rem(index + step, RING)


def neighbours(z, y, c, x):
    return {
        "sib": device(z, y, 1 - c, x),
        "zr": device(after(z, 1), y, c, x),
        "zl": device(after(z, 3), y, c, x),
        "yr": device(z, after(y, 1), c, x),
        "yl": device(z, after(y, 3), c, x),
    }


def greet(devices):
    barrier = pltpu.get_barrier_semaphore()
    for target in devices:
        pl.semaphore_signal(barrier, inc=1, device_id=target, device_id_type=MESH)
    pl.semaphore_wait(barrier, len(devices))


NT = (((1,), (1,)), ((), ()))
NN = (((1,), (0,)), ((), ()))
TN = (((0,), (0,)), ((), ()))


def dot(a, b, dims):
    return lax.dot_general(a, b, dims, preferred_element_type=jnp.float32)


def gather_kernel(
    keys, values, query, d_out, output, logsum,
    kz, vz, qz, gz, sz, qy, gy, ky, vy, sy, own_q, own_k, own_v, own_f,
    grad, outv, kv, vv, qv, stats, accq, acck, accv, fblk, accf, fout,
    send, recv, bulk_send, bulk_recv, local,
):
    z, y, c, x = place()
    near = neighbours(z, y, c, x)
    others = [((z * 4 + y) * 2 + c, after(x, step)) for step in (1, 2, 3)]
    greet(list(near.values()) + others)
    started = []

    def remote(index, src, dst, target):
        return pltpu.make_async_remote_copy(
            src_ref=src, dst_ref=dst, send_sem=send.at[index], recv_sem=recv.at[index],
            device_id=target, device_id_type=MESH,
        )

    def go(index, src, dst, target):
        copy = remote(index, src, dst, target)
        copy.start()
        started.append(copy)

    def bulk(array, kind, chunk, src, dst, target):
        return pltpu.make_async_remote_copy(
            src_ref=src, dst_ref=dst,
            send_sem=bulk_send.at[array * 7 + kind, chunk],
            recv_sem=bulk_recv.at[array * 7 + kind, chunk],
            device_id=target, device_id_type=MESH,
        )

    def spread(array, kind, src, head, dst, piece, target):
        for chunk in range(2):
            copy = bulk(
                array, kind, chunk,
                src.at[pl.ds(2 * chunk, 2), :, pl.ds(head * HD, HD)],
                dst.at[pl.ds(piece + 2 * chunk, 2)],
                target,
            )
            copy.start()
            started.append(copy)

    def relay(array, kind, ref, piece, *onward):
        for chunk in range(2):
            at = ref.at[pl.ds(piece + 2 * chunk, 2)]
            bulk(array, kind, chunk, at, at, near["sib"]).wait_recv()
            for kind_on, target in onward:
                copy = bulk(array, kind_on, chunk, at, at, target)
                copy.start()
                started.append(copy)

    def column(z_at, c_at):
        return (z_at * 2 + c_at) * BLK_DEV

    def row(y_at):
        return y_at * BLK_DEV

    def four(start):
        return pl.ds(start, BLK_DEV)

    zl, zr, zo = after(z, 3), after(z, 1), after(z, 2)
    yl, yr = after(y, 3), after(y, 1)
    top = (z == 0) & (y == 0)
    root = top & (c == 0)

    first_own = [
        pltpu.make_async_copy(keys.at[0], fblk.at[0], local.at[0]),
        pltpu.make_async_copy(values.at[0], fblk.at[1], local.at[1]),
    ]

    def first_copy(part, send_at, recv_at, target):
        return pltpu.make_async_remote_copy(
            src_ref=fblk.at[part], dst_ref=fblk.at[part],
            send_sem=send.at[send_at], recv_sem=recv.at[recv_at],
            device_id=target, device_id_type=MESH,
        )

    first_sends = [
        ((z == 0) & (y <= 1), first_copy(c, 28, 26, near["yr"])),
        ((z == 0) & (y == 0), first_copy(c, 29, 26, near["yl"])),
        (z <= 1, first_copy(c, 30, 26, near["zr"])),
        (z == 0, first_copy(c, 31, 26, near["zl"])),
        (jnp.logical_not(top & (c == 1)), first_copy(c, 32, 27, near["sib"])),
    ]
    first_start = first_copy(1, 33, 26, near["sib"])

    def send_first():
        for condition, copy in first_sends:
            @pl.when(condition)
            def _(copy=copy):
                copy.start()

    def pass_first(condition):
        @pl.when(condition)
        def _():
            first_copy(c, 28, 26, near["sib"]).wait_recv()
            send_first()

    @pl.when(root)
    def _():
        for copy in first_own:
            copy.start()
        for copy in first_own:
            copy.wait()
        first_start.start()
        send_first()

    pass_first(top & (c == 1))

    for step in (1, 2, 3):
        to = after(x, step)
        go(
            22 + step,
            d_out.at[:, pl.ds(pl.multiple_of(to * WIDTH, WIDTH), WIDTH)],
            grad.at[x],
            others[step - 1],
        )
    to_vmem = [
        pltpu.make_async_copy(
            d_out.at[:, pl.ds(pl.multiple_of(x * WIDTH, WIDTH), WIDTH)], grad.at[x], local.at[2]
        ),
        pltpu.make_async_copy(output, outv, local.at[3]),
        pltpu.make_async_copy(keys, kv, local.at[4]),
        pltpu.make_async_copy(values, vv, local.at[5]),
        pltpu.make_async_copy(query, qv, local.at[6]),
    ]
    kept = []
    for copy in to_vmem:
        copy.start()

    own_z, own_y = column(z, c), row(y)
    z_set = ((keys, 0, kz, 0), (values, 0, vz, 1), (query, 1, qz, 0), (grad, 1, gz, 1))
    y_set = ((query, 0, qy, 0), (grad, 0, gy, 1), (keys, 1, ky, 0), (values, 1, vy, 1))
    z_ways, y_ways = (near["zr"], near["zl"]), (near["yr"], near["yl"])

    def spread_all(kind, arrays):
        for array in arrays:
            if array < 4:
                src, head, ref, way = z_set[array]
                spread(array, kind, src, head, ref, own_z, z_ways[(way + kind) % 2])
            else:
                src, head, ref, way = y_set[array - 4]
                spread(array, kind, src, head, ref, own_y, y_ways[(way + kind) % 2])

    spread_all(0, (0, 1, 4, 7, 2, 6))
    spread_all(1, (0, 1, 4, 7, 2, 6))
    for array in (0, 1, 2):
        src, head, ref, _ = z_set[array]
        spread(array, 3, src, head, ref, own_z, near["sib"])

    pass_first((z == 0) & ((y == 1) | (y == 3)))
    to_vmem[0].wait()
    to_vmem[1].wait()
    for step in (1, 2, 3):
        remote(22 + step, grad.at[x], grad.at[x], others[step - 1]).wait_recv()
    spread_all(0, (3, 5))
    spread_all(1, (3, 5))
    spread(3, 3, grad, 1, gz, own_z, near["sib"])
    pass_first((z == 0) & (y == 2))
    stats[...] = jnp.zeros_like(stats)

    ones = jnp.ones((8, HD), jnp.bfloat16)
    for block in range(BLK_DEV):
        for head in range(2):
            part = pl.ds(head * HD, HD)
            product = grad[block, :, part].astype(jnp.float32) * outv[block, :, part].astype(jnp.float32)
            high = product.astype(jnp.bfloat16)
            low = (product - high.astype(jnp.float32)).astype(jnp.bfloat16)
            total = dot(ones, high, NT) + dot(ones, low, NT)
            stats[block, pl.ds(2 + head, 1), :] = total[0:1]
            stats[block, pl.ds(head, 1), :] = (
                logsum[pl.ds(head, 1), pl.ds(block * BLOCK, BLOCK)] * LOG2E
            )
    go(18, stats, sy.at[four(own_y)], near["yr"])
    go(19, stats, sy.at[four(own_y)], near["yl"])
    go(34, stats, sz.at[four(own_z)], near["zr"])
    go(35, stats, sz.at[four(own_z)], near["zl"])
    go(36, stats, sz.at[four(own_z)], near["sib"])

    for copy in to_vmem[2:]:
        copy.wait()
    held = {0: kv, 1: vv, 2: qv, 3: grad}
    keep = [(held[(0, 1, 2, 3)[at]], z_set[at][1], z_set[at][2].at[four(own_z)]) for at in range(4)]
    keep += [(held[(2, 3, 0, 1)[at]], y_set[at][1], y_set[at][2].at[four(own_y)]) for at in range(4)]
    keep += [(stats, None, sz.at[four(own_z)]), (stats, None, sy.at[four(own_y)])]
    for index, (src, head, dst) in enumerate(keep):
        part = src if head is None else src.at[:, :, pl.ds(head * HD, HD)]
        kept.append(pltpu.make_async_copy(part, dst, local.at[16 + index]))
        kept[-1].start()
    scale = 1.0 / math.sqrt(HD)

    def own_block(block, carry):
        for head in range(2):
            part = pl.ds(head * HD, HD)
            k, v, q, g = kv[block, :, part], vv[block, :, part], qv[block, :, part], grad[block, :, part]
            lse = stats[block, pl.ds(head, 1), :]
            delta = stats[block, pl.ds(2 + head, 1), :]
            p = jnp.exp2(dot(k, q, NT) * (scale * LOG2E) - lse)
            key_at = lax.broadcasted_iota(jnp.int32, (BLOCK, BLOCK), 0)
            query_at = lax.broadcasted_iota(jnp.int32, (BLOCK, BLOCK), 1)
            p = jnp.where(key_at <= query_at, p, 0.0)
            ds = (p * (dot(v, g, NT) - delta)).astype(jnp.bfloat16)
            accv[block, :, part] = dot(p.astype(jnp.bfloat16), g, NN)
            acck[block, :, part] = dot(ds, q, NN) * scale
            accq[block, :, part] = dot(ds, k, TN) * scale
        return carry

    def first_block(block, carry):
        for head in range(2):
            part = pl.ds(head * HD, HD)
            k, v, q, g = fblk[0, :, part], fblk[1, :, part], qv[block, :, part], grad[block, :, part]
            lse = stats[block, pl.ds(head, 1), :]
            delta = stats[block, pl.ds(2 + head, 1), :]
            p = jnp.exp2(dot(k, q, NT) * (scale * LOG2E) - lse)
            ds = (p * (dot(v, g, NT) - delta)).astype(jnp.bfloat16)
            accf[1, :, part] += dot(p.astype(jnp.bfloat16), g, NN)
            accf[0, :, part] += dot(ds, q, NN) * scale
            accq[block, :, part] += dot(ds, k, TN) * scale
        return carry

    lax.fori_loop(0, BLK_DEV, own_block, 0)
    for index, (src, dst) in enumerate(((acck, own_k), (accv, own_v))):
        kept.append(pltpu.make_async_copy(src, dst, local.at[12 + index]))
        kept[-1].start()
    pass_first((z == 1) | (z == 3))

    def pieces(array):
        if array < 4:
            _, _, ref, way = z_set[array]
            near_at, far_at = (zl, zr) if way == 0 else (zr, zl)
            return ref, [column(at, c) for at in (near_at, far_at, zo)], z_ways[way]
        _, _, ref, way = y_set[array - 4]
        near_at, far_at = (yl, yr) if way == 0 else (yr, yl)
        return ref, [row(at) for at in (near_at, far_at, after(y, 2))], y_ways[way]

    def onward(array, kind):
        ref, at, way = pieces(array)
        sends = [(2, way)] if kind == 0 else []
        if array < 4:
            sends.append((4 + kind, near["sib"]))
        relay(array, kind, ref, at[kind], *sends)

    for array in (0, 1, 4, 7, 2, 6):
        onward(array, 0)
    sy_in = [sy.at[four(row(after(y, step)))] for step in (3, 1, 2)]
    sz_in = [sz.at[four(column(after(z, step), c))] for step in (3, 1, 2)]

    def stat_in(index, ref):
        remote(index, ref, ref, near["sib"]).wait_recv()

    stat_in(18, sy_in[0])
    go(22, sy_in[0], sy_in[0], near["yr"])
    stat_in(34, sz_in[0])
    go(37, sz_in[0], sz_in[0], near["zr"])
    go(38, sz_in[0], sz_in[0], near["sib"])
    for array in (3, 5):
        onward(array, 0)
    pass_first(z == 2)

    @pl.when(jnp.logical_not(root))
    def _():
        first_copy(1 - c, 32, 27, near["sib"]).wait_recv()

    accf[...] = jnp.zeros_like(accf)
    lax.fori_loop(jnp.where(root, 1, 0), BLK_DEV, first_block, 0)
    fout[...] = accf[...].astype(jnp.bfloat16)
    for index, (src, dst) in enumerate(((accq, own_q), (fout, own_f))):
        kept.append(pltpu.make_async_copy(src, dst, local.at[14 + index]))
        kept[-1].start()
    stat_in(35, sz_in[1])
    go(39, sz_in[1], sz_in[1], near["sib"])
    for kind in (1, 2):
        for array in (0, 1, 4, 7, 2, 6, 3, 5):
            onward(array, kind)
    stat_in(37, sz_in[2])
    go(40, sz_in[2], sz_in[2], near["sib"])
    stat_in(19, sy_in[1])
    stat_in(22, sy_in[2])
    for array in range(4):
        ref, _, _ = pieces(array)
        way = z_set[array][3]
        order = (z, zl, zr, zo) if way == 0 else (z, zr, zl, zo)
        for kind, at in enumerate(order):
            relay(array, 3 + kind, ref, column(at, 1 - c))
    for index, at in ((36, z), (38, zl), (39, zr), (40, zo)):
        stat_in(index, sz.at[four(column(at, 1 - c))])
    for copy in kept:
        copy.wait()
    for copy in started:
        copy.wait_send()

    @pl.when(root)
    def _():
        first_start.wait_send()

    for condition, copy in first_sends:
        @pl.when(condition)
        def _(copy=copy):
            copy.wait_send()


def choose(selected, z, y, c, head):
    row_at = lax.broadcasted_iota(jnp.int32, (32, 1), 0)
    group, core, block = row_at >> 3, (row_at >> 2) & 1, row_at & 3
    if head == 0:
        slab = selected[pl.ds(pl.multiple_of(z * 32, 32), 32), :]
    else:
        slab = jnp.concatenate(
            [selected[pl.ds(pl.multiple_of(at * 32 + y * 8, 8), 8), :] for at in range(4)], axis=0
        )
    lane = lax.broadcasted_iota(jnp.int32, (32, 128), 1)
    found = jnp.zeros((32, 128), jnp.int32)
    for pick in range(3):
        chosen = slab[:, pick : pick + 1]
        z_of, y_of, c_of, b_of = chosen >> 5, (chosen >> 3) & 3, (chosen >> 2) & 1, chosen & 3
        if head == 0:
            here = (chosen > 0) & (y_of == y) & (core == c)
            target = ((z_of * 2 + c_of) * 4 + b_of) * 4 + group
            value = 1 + group * 4 + block
        else:
            here = (chosen > 0) & (z_of == z) & (c_of == c)
            target = (y_of * 4 + b_of) * 8 + group * 2 + core
            value = 1 + (group * 2 + core) * 4 + block
        found += jnp.where(here & (lane == target), value, 0)
    table = jnp.sum(found, axis=0, keepdims=True)
    down = lax.broadcasted_iota(jnp.int32, (128, 128), 0)
    across = lax.broadcasted_iota(jnp.int32, (128, 128), 1)
    spread = jnp.broadcast_to(table, (128, 128))
    rank = jnp.sum(jnp.where((across < down) & (spread > 0), 1, 0), axis=1, keepdims=True)
    entry = jnp.sum(jnp.where(across == down, spread, 0), axis=1, keepdims=True)
    item = jnp.where(entry > 0, down[:, 0:1] * 128 + entry, 0)
    items = jnp.sum(jnp.where(rank == across, item, 0), axis=0, keepdims=True)
    return items, table


def pair_kernel(
    selected, kz, vz, qz, gz, qy, gy, ky, vy, sz, sy,
    pz, py,
    lists_v, lists, kbuf, vbuf, qbuf, gbuf, dq0, dq1, dkv, kvout, qout0, qout1, zero,
    list_sem, in_sem, out_sem, q_sem, zero_sem,
):
    z, y, c, _ = place()
    scale = 1.0 / math.sqrt(HD)
    for head in range(2):
        items, table = choose(selected, z, y, c, head)
        lists_v[pl.ds(2 * head, 1), :] = items
        lists_v[pl.ds(2 * head + 1, 1), :] = table
    listed = pltpu.make_async_copy(lists_v, lists, list_sem)
    listed.start()
    zero[...] = jnp.zeros_like(zero)
    listed.wait()

    class Part:
        pass

    parts = []
    for head in range(2):
        part = Part()
        part.head, part.per, part.slots = head, (4, 8)[head], (32, 16)[head]
        part.k, part.v, part.q, part.g = ((kz, vz, qy, gy), (ky, vy, qz, gz))[head]
        part.stat, part.dq, part.qout = ((sy, dq0, qout0), (sz, dq1, qout1))[head]
        part.out, part.at = ((pz, 0), (py, 1))[head]
        part.dq_out, part.dq_at = ((py, 0), (pz, 2))[head]
        parts.append(part)

    def item_of(part, at):
        item = lists[2 * part.head, at]
        return lax.div(item, 128 * part.per), lax.rem(item, 128) - 1, item

    def loads(part, at):
        slot, block, _ = item_of(part, at)
        side = lax.rem(at, 2)
        pairs = ((part.k, kbuf, slot), (part.v, vbuf, slot), (part.q, qbuf, block), (part.g, gbuf, block))
        return [
            pltpu.make_async_copy(
                src.at[where], buf.at[part.head, side], in_sem.at[part.head, side, index]
            )
            for index, (src, buf, where) in enumerate(pairs)
        ]

    for part in parts:
        @pl.when(lists[2 * part.head, 0] > 0)
        def _(part=part):
            for copy in loads(part, 0):
                copy.start()

    def idle(part, slot):
        total = lists[2 * part.head + 1, slot * part.per]
        for at in range(1, part.per):
            total += lists[2 * part.head + 1, slot * part.per + at]
        return total == 0

    def blank(part, slot):
        return pltpu.make_async_copy(
            zero, part.out.at[slot, pl.ds(part.at, 2)], zero_sem.at[part.head, slot]
        )

    def each_idle(part, act):
        def one(slot, carry):
            @pl.when(idle(part, slot))
            def _():
                act(blank(part, slot))
            return carry

        lax.fori_loop(0, part.slots, one, 0)

    for part in parts:
        each_idle(part, lambda copy: copy.start())
        part.dq[...] = jnp.zeros_like(part.dq)

    out = pltpu.make_async_copy(kvout, pz.at[0, pl.ds(0, 2)], out_sem)
    written = 0
    for part in parts:
        def step(state, part=part):
            at, opened, done = state
            slot, block, _ = item_of(part, at)
            next_slot, _, following = item_of(part, at + 1)
            side = lax.rem(at, 2)

            @pl.when(following > 0)
            def _():
                for copy in loads(part, at + 1):
                    copy.start()

            for copy in loads(part, at):
                copy.wait()

            @pl.when(slot != opened)
            def _():
                dkv[...] = jnp.zeros_like(dkv)

            k, v = kbuf[part.head, side], vbuf[part.head, side]
            q, g = qbuf[part.head, side], gbuf[part.head, side]
            lse = part.stat[block, pl.ds(part.head, 1), :]
            delta = part.stat[block, pl.ds(2 + part.head, 1), :]
            p = jnp.exp2(dot(k, q, NT) * (scale * LOG2E) - lse)
            ds = (p * (dot(v, g, NT) - delta)).astype(jnp.bfloat16)
            dkv[1] += dot(p.astype(jnp.bfloat16), g, NN)
            dkv[0] += dot(ds, q, NN)
            part.dq[block] += dot(ds, k, TN)
            closing = (following == 0) | (next_slot != slot)

            @pl.when(closing)
            def _():
                @pl.when(done > 0)
                def _():
                    out.wait()
                kvout[0] = (dkv[0] * scale).astype(jnp.bfloat16)
                kvout[1] = dkv[1].astype(jnp.bfloat16)
                pltpu.make_async_copy(kvout, part.out.at[slot, pl.ds(part.at, 2)], out_sem).start()

            return at + 1, slot, done + jnp.where(closing, 1, 0)

        _, _, written = lax.while_loop(
            lambda state, part=part: lists[2 * part.head, state[0]] > 0,
            step,
            (jnp.int32(0), jnp.int32(-1), jnp.int32(written)),
        )

        def flush(block, part=part):
            return pltpu.make_async_copy(
                part.qout.at[block], part.dq_out.at[block, part.dq_at], q_sem.at[part.head, block]
            )

        def finish(block, carry, part=part, flush=flush):
            part.qout[block] = (part.dq[block] * scale).astype(jnp.bfloat16)
            flush(block).start()
            return carry

        part.flush = flush
        part.blocks = (16, 32)[part.head]
        lax.fori_loop(0, part.blocks, finish, 0)

    @pl.when(written > 0)
    def _():
        out.wait()

    for part in parts:
        def drain(block, carry, part=part):
            part.flush(block).wait()
            return carry

        lax.fori_loop(0, part.blocks, drain, 0)
        each_idle(part, lambda copy: copy.wait())


def scatter_kernel(
    pz, py, own_q, own_k, own_v, own_f,
    out_q, out_k, out_v,
    ownz, sibz, relz, finz, owny, rely, finy, accq, acck, accv,
    fown, frecv, fsum, fsend,
    send, recv, ring_send, ring_recv, local,
):
    z, y, c, x = place()
    near = neighbours(z, y, c, x)
    greet(list(near.values()))
    started = []

    def remote(index, src, dst, target):
        return pltpu.make_async_remote_copy(
            src_ref=src, dst_ref=dst, send_sem=send.at[index], recv_sem=recv.at[index],
            device_id=target, device_id_type=MESH,
        )

    def go(index, src, dst, target):
        copy = remote(index, src, dst, target)
        copy.start()
        started.append(copy)

    def came(index, dst):
        remote(index, dst, dst, near["sib"]).wait_recv()

    def ring_copy(index, src, dst, target):
        return pltpu.make_async_remote_copy(
            src_ref=src, dst_ref=dst, send_sem=ring_send.at[index], recv_sem=ring_recv.at[index],
            device_id=target, device_id_type=MESH,
        )

    def ring_go(index, src, dst, target):
        copy = ring_copy(index, src, dst, target)
        copy.start()
        started.append(copy)

    def ring_came(index, dst):
        ring_copy(index, dst, dst, near["sib"]).wait_recv()

    def column(z_at, c_at):
        return pl.ds((z_at * 2 + c_at) * BLK_DEV, BLK_DEV)

    def local_copy(index, src, dst):
        copy = pltpu.make_async_copy(src, dst, local.at[index])
        copy.start()
        return copy

    hops = (2, 1, 3, 0)
    locals_z, locals_y = [], []
    for j, hop in enumerate(hops):
        go(j, pz.at[column(after(z, hop), 1 - c)], sibz.at[j], near["sib"])
        locals_z.append(local_copy(j, pz.at[column(after(z, hop), c)], ownz.at[j]))
        locals_y.append(
            local_copy(4 + j, py.at[pl.ds(after(y, hop) * BLK_DEV, BLK_DEV)], owny.at[j])
        )
        if j == 0:
            remote(20, own_f.at[1 - c], frecv.at[0], near["sib"]).start()
            mine_f = local_copy(8, own_f.at[c], fown)
    locals_own = [
        local_copy(9 + j, src, dst)
        for j, (src, dst) in enumerate(((own_q, accq), (own_k, acck), (own_v, accv)))
    ]

    def add(dst, src):
        for part in range(3):
            dst[part] = (dst[part].astype(jnp.float32) + src[part].astype(jnp.float32)).astype(
                jnp.bfloat16
            )

    def merge(j):
        locals_z[j].wait()
        came(j, sibz.at[j])

        def one(block, carry):
            add(ownz.at[j, block], sibz.at[j, block])
            return carry

        lax.fori_loop(0, BLK_DEV, one, 0)

    rings = ((0, ownz, relz, finz, near["zr"], near["zl"]), (12, owny, rely, finy, near["yr"], near["yl"]))

    def ring_far(base, own, rel, fin, right, left):
        for block in range(2):
            ring_go(base + block, own.at[0, block], rel.at[0, block], right)
            ring_go(base + 2 + block, own.at[0, 2 + block], rel.at[1, block], left)

    def ring_right(base, own, rel, fin, right, left):
        for block in range(2):
            ring_go(base + 4 + block, own.at[1, 2 + block], fin.at[0, 2 + block], right)

    def ring_left(base, own, rel, fin, right, left):
        for block in range(2):
            ring_go(base + 6 + block, own.at[2, block], fin.at[1, block], left)

    def ring_relay(base, own, rel, fin, right, left):
        for block in range(2):
            ring_came(base + block, rel.at[0, block])
            add(own.at[1, block], rel.at[0, block])
            ring_go(base + 8 + block, own.at[1, block], fin.at[0, block], right)
            ring_came(base + 2 + block, rel.at[1, block])
            add(own.at[2, 2 + block], rel.at[1, block])
            ring_go(base + 10 + block, own.at[2, 2 + block], fin.at[1, 2 + block], left)

    def ring_end(base, own, rel, fin, right, left):
        for block in range(2):
            ring_came(base + 4 + block, fin.at[0, 2 + block])
            ring_came(base + 6 + block, fin.at[1, block])
            ring_came(base + 8 + block, fin.at[0, block])
            ring_came(base + 10 + block, fin.at[1, 2 + block])

    locals_y[0].wait()
    ring_far(*rings[1])
    merge(0)
    ring_far(*rings[0])

    f_sends = [
        ((y == 2) | (y == 1), remote(21, fsend.at[0], frecv.at[1], near["yl"])),
        (y == 3, remote(22, fsend.at[0], frecv.at[2], near["yr"])),
        ((y == 0) & ((z == 2) | (z == 1)), remote(23, fsend.at[1], frecv.at[3], near["zl"])),
        ((y == 0) & (z == 3), remote(24, fsend.at[1], frecv.at[4], near["zr"])),
    ]

    def f_take(at):
        came(20 + at, frecv.at[at])
        fsum[...] += frecv[at].astype(jnp.float32)

    def f_send(at):
        condition, copy = f_sends[at]

        @pl.when(condition)
        def _():
            fsend[at // 2] = fsum[...].astype(jnp.bfloat16)
            copy.start()

    mine_f.wait()
    came(20, frecv.at[0])
    fsum[...] = fown[...].astype(jnp.float32) + frecv[0].astype(jnp.float32)

    @pl.when(y == 1)
    def _():
        f_take(1)

    f_send(0)
    f_send(1)

    locals_y[1].wait()
    ring_right(*rings[1])
    locals_y[2].wait()
    ring_left(*rings[1])
    merge(1)
    ring_right(*rings[0])
    merge(2)
    ring_left(*rings[0])

    @pl.when(y == 0)
    def _():
        f_take(1)
        f_take(2)

        @pl.when(z == 1)
        def _():
            f_take(3)

    f_send(2)
    f_send(3)

    merge(3)
    ring_relay(*rings[1])
    ring_relay(*rings[0])
    top = (z == 0) & (y == 0)

    @pl.when(top)
    def _():
        f_take(3)
        f_take(4)

    locals_y[3].wait()
    for copy in locals_own:
        copy.wait()

    @pl.when(top & (c == 1))
    def _():
        fsend[1] = fsum[...].astype(jnp.bfloat16)
        remote(25, fsend.at[1], frecv.at[5], near["sib"]).start()

    @pl.when(top & (c == 0))
    def _():
        came(25, frecv.at[5])
        acck[0] += fsum[...]
        accv[0] += frecv[5].astype(jnp.float32)

    def total(own, fin, places):
        def one(block, carry):
            for part, (acc, out, head) in enumerate(places):
                lanes = pl.ds(head * HD, HD)
                value = acc[block, :, lanes]
                for ref in (own.at[3], fin.at[0], fin.at[1]):
                    value += ref[block, part].astype(jnp.float32)
                out[block, :, lanes] = value.astype(jnp.bfloat16)
            return carry

        lax.fori_loop(0, BLK_DEV, one, 0)

    ring_end(*rings[1])
    total(owny, finy, ((accq, out_q, 0), (acck, out_k, 1), (accv, out_v, 1)))
    ring_end(*rings[0])
    total(ownz, finz, ((acck, out_k, 0), (accv, out_v, 0), (accq, out_q, 1)))

    for copy in started:
        copy.wait_send()
    remote(20, fown, frecv.at[0], near["sib"]).wait_send()
    for condition, copy in f_sends + [
        (top & (c == 1), remote(25, fsend.at[1], frecv.at[5], near["sib"]))
    ]:
        @pl.when(condition)
        def _(copy=copy):
            copy.wait_send()


def body(query, keys, values, output, d_out, row_logsum, selected):
    bf16, f32 = jnp.bfloat16, jnp.float32
    any_spec = pl.BlockSpec(memory_space=pl.ANY)
    vmem_spec = pl.BlockSpec(memory_space=pltpu.VMEM)
    smem_spec = pl.BlockSpec(memory_space=pltpu.SMEM)
    blocked = (BLK_DEV, BLOCK, WIDTH)
    shape = jax.ShapeDtypeStruct
    dma, vmem, smem = pltpu.SemaphoreType.DMA, pltpu.VMEM, pltpu.SMEM
    zs, ys = shape((32, BLOCK, HD), bf16), shape((16, BLOCK, HD), bf16)
    kz, vz, qz, gz, sz, qy, gy, ky, vy, sy, own_q, own_k, own_v, own_f = pl.pallas_call(
        gather_kernel,
        out_shape=[zs] * 4
        + [shape((32, 8, BLOCK), f32)]
        + [ys] * 4
        + [shape((16, 8, BLOCK), f32)]
        + [shape(blocked, f32)] * 3
        + [shape((2, BLOCK, WIDTH), bf16)],
        in_specs=[any_spec] * 5 + [vmem_spec],
        out_specs=[any_spec] * 14,
        scratch_shapes=[vmem(blocked, bf16)] * 5
        + [vmem((BLK_DEV, 8, BLOCK), f32)]
        + [vmem(blocked, f32)] * 3
        + [
            vmem((2, BLOCK, WIDTH), bf16),
            vmem((2, BLOCK, WIDTH), f32),
            vmem((2, BLOCK, WIDTH), bf16),
            dma((41,)),
            dma((41,)),
            dma((56, 2)),
            dma((56, 2)),
            dma((26,)),
        ],
        compiler_params=pltpu.CompilerParams(
            collective_id=0, has_side_effects=True, vmem_limit_bytes=VMEM
        ),
        name="gather",
    )(
        keys.reshape(blocked), values.reshape(blocked), query.reshape(blocked),
        d_out, output.reshape(blocked), row_logsum,
    )
    pz, py = pl.pallas_call(
        pair_kernel,
        out_shape=[shape((32, 3, BLOCK, HD), bf16), shape((16, 3, BLOCK, HD), bf16)],
        in_specs=[vmem_spec] + [any_spec] * 8 + [vmem_spec] * 2,
        out_specs=[any_spec] * 2,
        scratch_shapes=[
            vmem((8, 128), jnp.int32),
            smem((8, 128), jnp.int32),
            vmem((2, 2, BLOCK, HD), bf16),
            vmem((2, 2, BLOCK, HD), bf16),
            vmem((2, 2, BLOCK, HD), bf16),
            vmem((2, 2, BLOCK, HD), bf16),
            vmem((16, BLOCK, HD), f32),
            vmem((32, BLOCK, HD), f32),
            vmem((2, BLOCK, HD), f32),
            vmem((2, BLOCK, HD), bf16),
            vmem((16, BLOCK, HD), bf16),
            vmem((32, BLOCK, HD), bf16),
            vmem((2, BLOCK, HD), bf16),
            dma,
            dma((2, 2, 4)),
            dma,
            dma((2, 32)),
            dma((2, 32)),
        ],
        compiler_params=pltpu.CompilerParams(vmem_limit_bytes=VMEM),
        name="pairs",
    )(selected, kz, vz, qz, gz, qy, gy, ky, vy, sz, sy)
    piece = (BLK_DEV, 3, BLOCK, HD)
    out_q, out_k, out_v = pl.pallas_call(
        scatter_kernel,
        out_shape=[shape(blocked, bf16)] * 3,
        in_specs=[any_spec] * 6,
        out_specs=[vmem_spec] * 3,
        scratch_shapes=[
            vmem((4,) + piece, bf16),
            vmem((4,) + piece, bf16),
            vmem((2, 2, 3, BLOCK, HD), bf16),
            vmem((2,) + piece, bf16),
            vmem((4,) + piece, bf16),
            vmem((2, 2, 3, BLOCK, HD), bf16),
            vmem((2,) + piece, bf16),
            vmem(blocked, f32),
            vmem(blocked, f32),
            vmem(blocked, f32),
            vmem((BLOCK, WIDTH), bf16),
            vmem((6, BLOCK, WIDTH), bf16),
            vmem((BLOCK, WIDTH), f32),
            vmem((2, BLOCK, WIDTH), bf16),
            dma((26,)),
            dma((26,)),
            dma((24,)),
            dma((24,)),
            dma((12,)),
        ],
        compiler_params=pltpu.CompilerParams(
            collective_id=1, has_side_effects=True, vmem_limit_bytes=VMEM
        ),
        name="scatter",
    )(pz, py, own_q, own_k, own_v, own_f)
    flat = (BLK_DEV * BLOCK, WIDTH)
    return out_q.reshape(flat), out_k.reshape(flat), out_v.reshape(flat)


def solution(mesh):
    in_specs = (
        P("seq", "head"),
        P("seq", "head"),
        P("seq", "head"),
        P("seq", "head"),
        P(("seq", "head"), None),
        P("head", "seq"),
        P(),
    )
    out_specs = (P("seq", "head"), P("seq", "head"), P("seq", "head"))
    return jax.shard_map(body, mesh=mesh, in_specs=in_specs, out_specs=out_specs, check_vma=False)
```

time: 225 us -> 204 us (0.907)
  Pallas kernels: 217 us -> 197 us
    pallas_call x1, Pallas kernels: 113 us -> 80.2 us  [body(): pl.pallas_call(scatter_kernel, out_shape=[shape(blocked, bf16)] * 3, in_s...]
    pallas_call x2, Pallas kernels: 104 us -> 116 us  [the longest x1 85.1 us: body(): pl.pallas_call(gather_kernel, out_shape=[zs] * 4 + [shape((32, 8, BLOCK),...]
    unnamed x6 -> x8, local copies, waits for them, and re-layouts: 6.37 us -> 5.77 us
where the time goes in v4:
time: 204 us; the launch traced here: 203 us
  Pallas kernels  197 us (97%)
  local copies, waits for them, and re-layouts  5.77 us (3%)
    pallas_call x1, Pallas kernels, body(): pl.pallas_call(gather_kernel, out_shape=[zs] * 4 + [shape((32, 8, BLOCK),...  85.1 us
    pallas_call x1, Pallas kernels, body(): pl.pallas_call(scatter_kernel, out_shape=[shape(blocked, bf16)] * 3, in_s...  80.2 us
    pallas_call x1, Pallas kernels, body(): pl.pallas_call(pair_kernel, out_shape=[shape((32, 3, BLOCK, HD), bf16), s...  31.3 us
    unnamed x8, local copies, waits for them, and re-layouts  5.77 us

profile of v4, /device:TPU:0, one launch (start us, length us, event | category | flops | bytes accessed | tf_op | source)
XLA Modules:
  0.0 203.1 jit_solution(11440167775546184251)
XLA Ops:
  0.6 1.4 copy.10.selected
  2.0 85.1 %gather.1 = (bf16[32,512,128]{2,1,0:T(8,128)(2,1)}, bf16[32,512,128]{2,1,0:T(8,128)(2,1)}, bf16[32,512,128]{2,1,0:T(8,128)(2,1)}, bf16[32,512,128]{2,1,0:T(8,128...) custom-call(bf16[4,512,256]{2,1,0:T(8,128)(2,1)} %bitcast.7, ...), custom_call_target="tpu_custom_call" | custom-call | tf_op jit(solution)/shard_map/gather/pallas_call | solution.py:776
  87.1 31.3 %pairs.1 = (bf16[32,3,512,128]{3,2,1,0:T(8,128)(2,1)}, bf16[16,3,512,128]{3,2,1,0:T(8,128)(2,1)}) custom-call(s32[128,3]{1,0:T(8,128)} %copy.10.selected, bf16[32,512,128]{2,1,0:T(8,128)(2,1)} %get-tuple-element.22.kz, bf16[32,512,128]{2,1,0:T(8,128)(2,1)} %get-tuple-element.23.vz, bf16[32,512,128]{2,1,0:T(8,128)(2,1)} %get-tuple-element.24.qz, ...), custom_call_target="tpu_custom_call" | custom-call | tf_op jit(solution)/shard_map/pairs/pallas_call | solution.py:807
  118.5 80.2 %scatter.1 = (bf16[4,512,256]{2,1,0:T(8,128)(2,1)}, bf16[4,512,256]{2,1,0:T(8,128)(2,1)}, bf16[4,512,256]{2,1,0:T(8,128)(2,1)}) custom-call(bf16[32,3,512,128]{3,2,1,0:T(8,128)(2,1)} %get-tuple-element.32.pz, bf16[16,3,512,128]{3,2,1,0:T(8,128)(2,1)} %get-tuple-element.33.py, f32[4,512,256]{2,1,0:T(8,128)} %get-tuple-element.34.own_q, ...), custom_call_target="tpu_custom_call" | custom-call | tf_op jit(solution)/shard_map/scatter/pallas_call | solution.py:836
  198.7 0.0 copy-start.1
  198.7 0.0 copy-start
  198.7 2.4 %copy.14 = bf16[2048,256]{1,0:T(8,128)(2,1)} copy(bf16[2048,256]{1,0:T(8,128)(2,1)} %bitcast.13) | data formatting | bytes 2097152
  201.1 0.0 copy-done.1
  201.1 1.0 copy.15
  202.1 0.0 copy-done
  202.1 1.0 copy.16
Async XLA Ops:
  198.7 2.4 %copy-start.1 = (bf16[4,512,256]{2,1,0:T(8,128)(2,1)S(1)}, bf16[4,512,256]{2,1,0:T(8,128)(2,1)}, u32[]{:S(2)}) copy-start(bf16[4,512,256]{2,1,0:T(8,128)(2,1)} %get-tuple-element.39) | copy-start | bytes 3145732
  198.7 3.4 %copy-start = (bf16[4,512,256]{2,1,0:T(8,128)(2,1)S(1)}, bf16[4,512,256]{2,1,0:T(8,128)(2,1)}, u32[]{:S(2)}) copy-start(bf16[4,512,256]{2,1,0:T(8,128)(2,1)} %get-tuple-element.40) | copy-start | bytes 3145732

commit v5 on v4

--- a/solution.py
+++ b/solution.py
@@ -89,25 +89,37 @@
             device_id=target, device_id_type=MESH,
         )
 
-    def spread(array, kind, src, head, dst, piece, target):
-        for chunk in range(2):
-            copy = bulk(
+    started_if = []
+
+    def start_if(condition, copies):
+        @pl.when(condition)
+        def _():
+            for copy in copies:
+                copy.start()
+
+        started_if.append((condition, copies))
+
+    def spread(array, kind, src, head, dst, piece, target, condition):
+        start_if(condition, [
+            bulk(
                 array, kind, chunk,
                 src.at[pl.ds(2 * chunk, 2), :, pl.ds(head * HD, HD)],
                 dst.at[pl.ds(piece + 2 * chunk, 2)],
                 target,
             )
-            copy.start()
-            started.append(copy)
-
-    def relay(array, kind, ref, piece, *onward):
+            for chunk in range(2)
+        ])
+
+    def relay(array, kind, ref, piece, condition, *onward):
         for chunk in range(2):
             at = ref.at[pl.ds(piece + 2 * chunk, 2)]
-            bulk(array, kind, chunk, at, at, near["sib"]).wait_recv()
-            for kind_on, target in onward:
-                copy = bulk(array, kind_on, chunk, at, at, target)
-                copy.start()
-                started.append(copy)
+
+            @pl.when(condition)
+            def _(at=at, chunk=chunk):
+                bulk(array, kind, chunk, at, at, near["sib"]).wait_recv()
+
+            for kind_on, target, condition_on in onward:
+                start_if(condition_on, [bulk(array, kind_on, chunk, at, at, target)])
 
     def column(z_at, c_at):
         return (z_at * 2 + c_at) * BLK_DEV
@@ -193,20 +205,37 @@
     y_set = ((query, 0, qy, 0), (grad, 0, gy, 1), (keys, 1, ky, 0), (values, 1, vy, 1))
     z_ways, y_ways = (near["zr"], near["zl"]), (near["yr"], near["yl"])
 
+    def wanted(array, src, dst):
+        if array < 2:
+            return dst > src
+        if array < 4:
+            return dst < src
+        if array < 6:
+            return (dst < src) | (z > 0)
+        return (dst > src) | (z < 3)
+
+    def sent(array, kind, src):
+        way = (z_set + y_set)[array][3]
+        step = (1, 3)[way]
+        if kind == 0:
+            return wanted(array, src, after(src, step)) | wanted(array, src, after(src, 2))
+        if kind == 1:
+            return wanted(array, src, after(src, 4 - step))
+        return wanted(array, src, after(src, 2))
+
     def spread_all(kind, arrays):
         for array in arrays:
-            if array < 4:
-                src, head, ref, way = z_set[array]
-                spread(array, kind, src, head, ref, own_z, z_ways[(way + kind) % 2])
-            else:
-                src, head, ref, way = y_set[array - 4]
-                spread(array, kind, src, head, ref, own_y, y_ways[(way + kind) % 2])
+            src, head, ref, way = (z_set + y_set)[array]
+            piece, at, ways = (own_z, z, z_ways) if array < 4 else (own_y, y, y_ways)
+            spread(
+                array, kind, src, head, ref, piece, ways[(way + kind) % 2], sent(array, kind, at)
+            )
 
     spread_all(0, (0, 1, 4, 7, 2, 6))
     spread_all(1, (0, 1, 4, 7, 2, 6))
     for array in (0, 1, 2):
         src, head, ref, _ = z_set[array]
-        spread(array, 3, src, head, ref, own_z, near["sib"])
+        spread(array, 3, src, head, ref, own_z, near["sib"], z >= 0)
 
     pass_first((z == 0) & ((y == 1) | (y == 3)))
     to_vmem[0].wait()
@@ -215,7 +244,7 @@
         remote(22 + step, grad.at[x], grad.at[x], others[step - 1]).wait_recv()
     spread_all(0, (3, 5))
     spread_all(1, (3, 5))
-    spread(3, 3, grad, 1, gz, own_z, near["sib"])
+    spread(3, 3, grad, 1, gz, own_z, near["sib"], z >= 0)
     pass_first((z == 0) & (y == 2))
     stats[...] = jnp.zeros_like(stats)
 
@@ -285,20 +314,20 @@
     pass_first((z == 1) | (z == 3))
 
     def pieces(array):
+        _, _, ref, way = (z_set + y_set)[array]
         if array < 4:
-            _, _, ref, way = z_set[array]
-            near_at, far_at = (zl, zr) if way == 0 else (zr, zl)
-            return ref, [column(at, c) for at in (near_at, far_at, zo)], z_ways[way]
-        _, _, ref, way = y_set[array - 4]
-        near_at, far_at = (yl, yr) if way == 0 else (yr, yl)
-        return ref, [row(at) for at in (near_at, far_at, after(y, 2))], y_ways[way]
+            at = (zl, zr, zo) if way == 0 else (zr, zl, zo)
+            return ref, at, [column(one, c) for one in at], z_ways[way]
+        at = (yl, yr, after(y, 2)) if way == 0 else (yr, yl, after(y, 2))
+        return ref, at, [row(one) for one in at], y_ways[way]
 
     def onward(array, kind):
-        ref, at, way = pieces(array)
-        sends = [(2, way)] if kind == 0 else []
+        ref, at, piece, way = pieces(array)
+        came = sent(array, kind, at[kind])
+        sends = [(2, way, sent(array, 2, at[0]))] if kind == 0 else []
         if array < 4:
-            sends.append((4 + kind, near["sib"]))
-        relay(array, kind, ref, at[kind], *sends)
+            sends.append((4 + kind, near["sib"], came))
+        relay(array, kind, ref, piece[kind], came, *sends)
 
     for array in (0, 1, 4, 7, 2, 6):
         onward(array, 0)
@@ -337,15 +366,20 @@
     stat_in(19, sy_in[1])
     stat_in(22, sy_in[2])
     for array in range(4):
-        ref, _, _ = pieces(array)
-        way = z_set[array][3]
-        order = (z, zl, zr, zo) if way == 0 else (z, zr, zl, zo)
-        for kind, at in enumerate(order):
-            relay(array, 3 + kind, ref, column(at, 1 - c))
+        ref, at, _, _ = pieces(array)
+        relay(array, 3, ref, column(z, 1 - c), z >= 0)
+        for kind in range(3):
+            relay(array, 4 + kind, ref, column(at[kind], 1 - c), sent(array, kind, at[kind]))
     for index, at in ((36, z), (38, zl), (39, zr), (40, zo)):
         stat_in(index, sz.at[four(column(at, 1 - c))])
     for copy in kept:
         copy.wait()
+    for condition, copies in started_if:
+        @pl.when(condition)
+        def _(copies=copies):
+            for copy in copies:
+                copy.wait_send()
+
     for copy in started:
         copy.wait_send()
 
@@ -762,6 +796,26 @@
         @pl.when(condition)
         def _(copy=copy):
             copy.wait_send()
+
+
+def keep_kernel(in_q, in_k, in_v, out_q, out_k, out_v, held, in_sem, out_sem):
+    ins, outs = [], []
+    for part, (src, dst) in enumerate(((in_q, out_q), (in_k, out_k), (in_v, out_v))):
+        for half in range(2):
+            piece = pl.ds(2 * half, 2)
+            ins.append(
+                pltpu.make_async_copy(src.at[piece], held.at[part, piece], in_sem.at[part, half])
+            )
+            outs.append(
+                pltpu.make_async_copy(held.at[part, piece], dst.at[piece], out_sem.at[part, half])
+            )
+    for copy in ins:
+        copy.start()
+    for copy, out in zip(ins, outs):
+        copy.wait()
+        out.start()
+    for out in outs:
+        out.wait()
 
 
 def body(query, keys, values, output, d_out, row_logsum, selected):
@@ -864,6 +918,15 @@
         ),
         name="scatter",
     )(pz, py, own_q, own_k, own_v, own_f)
+    out_q, out_k, out_v = pl.pallas_call(
+        keep_kernel,
+        out_shape=[shape(blocked, bf16)] * 3,
+        in_specs=[any_spec] * 3,
+        out_specs=[any_spec] * 3,
+        scratch_shapes=[vmem((3,) + blocked, bf16), dma((3, 2)), dma((3, 2))],
+        compiler_params=pltpu.CompilerParams(vmem_limit_bytes=VMEM),
+        name="keep",
+    )(out_q, out_k, out_v)
     flat = (BLK_DEV * BLOCK, WIDTH)
     return out_q.reshape(flat), out_k.reshape(flat), out_v.reshape(flat)
 

time: 204 us -> 198 us (0.971); the launches traced: 203 us -> 195 us
  Pallas kernels: 197 us -> 192 us
  local copies, waits for them, and re-layouts: 5.77 us -> 1.42 us
    pallas_call x1, Pallas kernels: 80.2 us -> 74.3 us  [body(): pl.pallas_call(scatter_kernel, out_shape=[shape(blocked, bf16)] * 3, in_s...]
    unnamed x8 -> x1, local copies, waits for them, and re-layouts: 5.77 us -> 1.42 us
    pallas_call x0 -> x1, Pallas kernels: none -> 2.8 us  [body(): pl.pallas_call(keep_kernel, out_shape=[shape(blocked, bf16)] * 3, in_spec...]
where the time goes in v5:
time: 198 us; the launch traced here: 195 us
  Pallas kernels  192 us (97%)
    pallas_call x1, Pallas kernels, body(): pl.pallas_call(gather_kernel, out_shape=[zs] * 4 + [shape((32, 8, BLOCK),...  83.1 us
    pallas_call x1, Pallas kernels, body(): pl.pallas_call(scatter_kernel, out_shape=[shape(blocked, bf16)] * 3, in_s...  74.3 us
    pallas_call x1, Pallas kernels, body(): pl.pallas_call(pair_kernel, out_shape=[shape((32, 3, BLOCK, HD), bf16), s...  32.3 us

profile of v5, /device:TPU:0, one launch (start us, length us, event | category | flops | bytes accessed | tf_op | source)
XLA Modules:
  0.0 194.6 jit_solution(10722386709757678205)
XLA Ops:
  0.6 1.4 copy.10.selected
  2.0 83.1 %gather.1 = (bf16[32,512,128]{2,1,0:T(8,128)(2,1)}, bf16[32,512,128]{2,1,0:T(8,128)(2,1)}, bf16[32,512,128]{2,1,0:T(8,128)(2,1)}, bf16[32,512,128]{2,1,0:T(8,128...) custom-call(bf16[4,512,256]{2,1,0:T(8,128)(2,1)} %bitcast.7, ...), custom_call_target="tpu_custom_call" | custom-call | tf_op jit(solution)/shard_map/gather/pallas_call | solution.py:830
  85.1 32.3 %pairs.1 = (bf16[32,3,512,128]{3,2,1,0:T(8,128)(2,1)}, bf16[16,3,512,128]{3,2,1,0:T(8,128)(2,1)}) custom-call(s32[128,3]{1,0:T(8,128)} %copy.10.selected, bf16[32,512,128]{2,1,0:T(8,128)(2,1)} %get-tuple-element.25.kz, bf16[32,512,128]{2,1,0:T(8,128)(2,1)} %get-tuple-element.26.vz, bf16[32,512,128]{2,1,0:T(8,128)(2,1)} %get-tuple-element.27.qz, ...), custom_call_target="tpu_custom_call" | custom-call | tf_op jit(solution)/shard_map/pairs/pallas_call | solution.py:861
  117.5 74.3 %scatter.1 = (bf16[4,512,256]{2,1,0:T(8,128)(2,1)}, bf16[4,512,256]{2,1,0:T(8,128)(2,1)}, bf16[4,512,256]{2,1,0:T(8,128)(2,1)}) custom-call(bf16[32,3,512,128]{3,2,1,0:T(8,128)(2,1)} %get-tuple-element.35.pz, bf16[16,3,512,128]{3,2,1,0:T(8,128)(2,1)} %get-tuple-element.36.py, f32[4,512,256]{2,1,0:T(8,128)} %get-tuple-element.37.own_q, ...), custom_call_target="tpu_custom_call" | custom-call | tf_op jit(solution)/shard_map/scatter/pallas_call | solution.py:890
  191.8 2.8 %keep.1 = (bf16[4,512,256]{2,1,0:T(8,128)(2,1)}, bf16[4,512,256]{2,1,0:T(8,128)(2,1)}, bf16[4,512,256]{2,1,0:T(8,128)(2,1)}) custom-call(bf16[4,512,256]{2,1,0:T(8,128)(2,1)} %get-tuple-element.41.in_q, bf16[4,512,256]{2,1,0:T(8,128)(2,1)} %get-tuple-element.42.in_k, bf16[4,512,256]{2,1,0:T(8,128)(2,1)} %get-tuple-element.43.in_v), custom_call_target="tpu_custom_call" | custom-call | tf_op jit(solution)/shard_map/keep/pallas_call | solution.py:921

commit v6 on v5

--- a/solution.py
+++ b/solution.py
@@ -442,6 +442,8 @@
     listed = pltpu.make_async_copy(lists_v, lists, list_sem)
     listed.start()
     zero[...] = jnp.zeros_like(zero)
+    dq0[...] = jnp.zeros_like(dq0)
+    dq1[...] = jnp.zeros_like(dq1)
     listed.wait()
 
     class Part:
@@ -500,56 +502,85 @@
 
     for part in parts:
         each_idle(part, lambda copy: copy.start())
-        part.dq[...] = jnp.zeros_like(part.dq)
-
-    out = pltpu.make_async_copy(kvout, pz.at[0, pl.ds(0, 2)], out_sem)
-    written = 0
+
+    def put(part, slot):
+        return pltpu.make_async_copy(
+            kvout.at[part.head], part.out.at[slot, pl.ds(part.at, 2)], out_sem.at[part.head]
+        )
+
+    def enter(part, at, opened):
+        slot, _, _ = item_of(part, at)
+        _, _, following = item_of(part, at + 1)
+
+        @pl.when(following > 0)
+        def _():
+            for copy in loads(part, at + 1):
+                copy.start()
+
+        for copy in loads(part, at):
+            copy.wait()
+
+        @pl.when(slot != opened)
+        def _():
+            dkv[part.head] = jnp.zeros(dkv.shape[1:], dkv.dtype)
+
+    def work(part, at):
+        _, block, _ = item_of(part, at)
+        side = lax.rem(at, 2)
+        k, v = kbuf[part.head, side], vbuf[part.head, side]
+        q, g = qbuf[part.head, side], gbuf[part.head, side]
+        lse = part.stat[block, pl.ds(part.head, 1), :]
+        delta = part.stat[block, pl.ds(2 + part.head, 1), :]
+        p = jnp.exp2(dot(k, q, NT) * (scale * LOG2E) - lse)
+        ds = (p * (dot(v, g, NT) - delta)).astype(jnp.bfloat16)
+        dkv[part.head, 1] += dot(p.astype(jnp.bfloat16), g, NN)
+        dkv[part.head, 0] += dot(ds, q, NN)
+        part.dq[block] += dot(ds, k, TN)
+
+    def leave(part, at, done):
+        slot, _, _ = item_of(part, at)
+        next_slot, _, following = item_of(part, at + 1)
+        closing = (following == 0) | (next_slot != slot)
+
+        @pl.when(closing)
+        def _():
+            @pl.when(done > 0)
+            def _():
+                put(part, 0).wait()
+            kvout[part.head, 0] = (dkv[part.head, 0] * scale).astype(jnp.bfloat16)
+            kvout[part.head, 1] = dkv[part.head, 1].astype(jnp.bfloat16)
+            put(part, slot).start()
+
+        return slot, done + jnp.where(closing, 1, 0)
+
+    def both(state):
+        at, opened0, done0, opened1, done1 = state
+        enter(parts[0], at, opened0)
+        enter(parts[1], at, opened1)
+        work(parts[0], at)
+        work(parts[1], at)
+        return (at + 1,) + leave(parts[0], at, done0) + leave(parts[1], at, done1)
+
+    none, nil = jnp.int32(-1), jnp.int32(0)
+    at_both, *rest = lax.while_loop(
+        lambda state: (lists[0, state[0]] > 0) & (lists[2, state[0]] > 0),
+        both,
+        (nil, none, nil, none, nil),
+    )
+    ends = []
     for part in parts:
-        def step(state, part=part):
+        def one(state, part=part):
             at, opened, done = state
-            slot, block, _ = item_of(part, at)
-            next_slot, _, following = item_of(part, at + 1)
-            side = lax.rem(at, 2)
-
-            @pl.when(following > 0)
-            def _():
-                for copy in loads(part, at + 1):
-                    copy.start()
-
-            for copy in loads(part, at):
-                copy.wait()
-
-            @pl.when(slot != opened)
-            def _():
-                dkv[...] = jnp.zeros_like(dkv)
-
-            k, v = kbuf[part.head, side], vbuf[part.head, side]
-            q, g = qbuf[part.head, side], gbuf[part.head, side]
-            lse = part.stat[block, pl.ds(part.head, 1), :]
-            delta = part.stat[block, pl.ds(2 + part.head, 1), :]
-            p = jnp.exp2(dot(k, q, NT) * (scale * LOG2E) - lse)
-            ds = (p * (dot(v, g, NT) - delta)).astype(jnp.bfloat16)
-            dkv[1] += dot(p.astype(jnp.bfloat16), g, NN)
-            dkv[0] += dot(ds, q, NN)
-            part.dq[block] += dot(ds, k, TN)
-            closing = (following == 0) | (next_slot != slot)
-
-            @pl.when(closing)
-            def _():
-                @pl.when(done > 0)
-                def _():
-                    out.wait()
-                kvout[0] = (dkv[0] * scale).astype(jnp.bfloat16)
-                kvout[1] = dkv[1].astype(jnp.bfloat16)
-                pltpu.make_async_copy(kvout, part.out.at[slot, pl.ds(part.at, 2)], out_sem).start()
-
-            return at + 1, slot, done + jnp.where(closing, 1, 0)
-
-        _, _, written = lax.while_loop(
+            enter(part, at, opened)
+            work(part, at)
+            return (at + 1,) + leave(part, at, done)
+
+        _, _, done = lax.while_loop(
             lambda state, part=part: lists[2 * part.head, state[0]] > 0,
-            step,
-            (jnp.int32(0), jnp.int32(-1), jnp.int32(written)),
+            one,
+            (at_both, rest[2 * part.head], rest[2 * part.head + 1]),
         )
+        ends.append(done)
 
         def flush(block, part=part):
             return pltpu.make_async_copy(
@@ -565,9 +596,10 @@
         part.blocks = (16, 32)[part.head]
         lax.fori_loop(0, part.blocks, finish, 0)
 
-    @pl.when(written > 0)
-    def _():
-        out.wait()
+    for part in parts:
+        @pl.when(ends[part.head] > 0)
+        def _(part=part):
+            put(part, 0).wait()
 
     for part in parts:
         def drain(block, carry, part=part):
@@ -587,8 +619,11 @@
 ):
     z, y, c, x = place()
     near = neighbours(z, y, c, x)
+    relz[...] = jnp.zeros_like(relz)
+    finz[...] = jnp.zeros_like(finz)
     greet(list(near.values()))
     started = []
+    started_if = []
 
     def remote(index, src, dst, target):
         return pltpu.make_async_remote_copy(
@@ -604,19 +639,45 @@
     def came(index, dst):
         remote(index, dst, dst, near["sib"]).wait_recv()
 
-    def ring_copy(index, src, dst, target):
-        return pltpu.make_async_remote_copy(
-            src_ref=src, dst_ref=dst, send_sem=ring_send.at[index], recv_sem=ring_recv.at[index],
-            device_id=target, device_id_type=MESH,
-        )
-
-    def ring_go(index, src, dst, target):
-        copy = ring_copy(index, src, dst, target)
-        copy.start()
-        started.append(copy)
-
-    def ring_came(index, dst):
-        ring_copy(index, dst, dst, near["sib"]).wait_recv()
+    def ring_copies(index, src, dst, target, groups):
+        copies = []
+        for at, (condition, first, size) in enumerate(groups):
+            part = pl.ds(first, size)
+            copies.append((condition, pltpu.make_async_remote_copy(
+                src_ref=src.at[part], dst_ref=dst.at[part],
+                send_sem=ring_send.at[index, at], recv_sem=ring_recv.at[index, at],
+                device_id=target, device_id_type=MESH,
+            )))
+        return copies
+
+    def ring_go(index, src, dst, target, groups):
+        for condition, copy in ring_copies(index, src, dst, target, groups):
+            @pl.when(condition)
+            def _(copy=copy):
+                copy.start()
+
+            started_if.append((condition, copy))
+
+    def ring_came(index, dst, groups):
+        for condition, copy in ring_copies(index, dst, dst, near["sib"], groups):
+            @pl.when(condition)
+            def _(copy=copy):
+                copy.wait_recv()
+
+    def whole(_):
+        return [(z >= 0, 0, 3)]
+
+    def split(low, high):
+        return [(low, 0, 2), (high, 2, 1)]
+
+    y_kinds = {kind: whole for kind in ("far", "right", "left", "on_right", "on_left")}
+    z_kinds = {
+        "far": lambda at: split(at >= 2, at < 2),
+        "right": lambda at: split(at == 3, at < 3),
+        "left": lambda at: split(at > 0, at == 0),
+        "on_right": lambda at: split((at == 0) | (at == 3), at < 3),
+        "on_left": lambda at: split(at > 0, (at == 0) | (at == 3)),
+    }
 
     def column(z_at, c_at):
         return pl.ds((z_at * 2 + c_at) * BLK_DEV, BLK_DEV)
@@ -658,36 +719,47 @@
 
         lax.fori_loop(0, BLK_DEV, one, 0)
 
-    rings = ((0, ownz, relz, finz, near["zr"], near["zl"]), (12, owny, rely, finy, near["yr"], near["yl"]))
-
-    def ring_far(base, own, rel, fin, right, left):
+    rings = (
+        (0, ownz, relz, finz, near["zr"], near["zl"], z, z_kinds),
+        (12, owny, rely, finy, near["yr"], near["yl"], y, y_kinds),
+    )
+
+    def ring_far(base, own, rel, fin, right, left, me, kinds):
+        groups = kinds["far"](me)
         for block in range(2):
-            ring_go(base + block, own.at[0, block], rel.at[0, block], right)
-            ring_go(base + 2 + block, own.at[0, 2 + block], rel.at[1, block], left)
-
-    def ring_right(base, own, rel, fin, right, left):
+            ring_go(base + block, own.at[0, block], rel.at[0, block], right, groups)
+            ring_go(base + 2 + block, own.at[0, 2 + block], rel.at[1, block], left, groups)
+
+    def ring_right(base, own, rel, fin, right, left, me, kinds):
+        for block in range(2, 4):
+            ring_go(base + 2 + block, own.at[1, block], fin.at[0, block], right, kinds["right"](me))
+
+    def ring_left(base, own, rel, fin, right, left, me, kinds):
         for block in range(2):
-            ring_go(base + 4 + block, own.at[1, 2 + block], fin.at[0, 2 + block], right)
-
-    def ring_left(base, own, rel, fin, right, left):
+            ring_go(base + 6 + block, own.at[2, block], fin.at[1, block], left, kinds["left"](me))
+
+    def ring_relay(base, own, rel, fin, right, left, me, kinds):
+        before, behind = after(me, 3), after(me, 1)
         for block in range(2):
-            ring_go(base + 6 + block, own.at[2, block], fin.at[1, block], left)
-
-    def ring_relay(base, own, rel, fin, right, left):
+            ring_came(base + block, rel.at[0, block], kinds["far"](before))
+            add(own.at[1, block], rel.at[0, block])
+            ring_go(
+                base + 8 + block, own.at[1, block], fin.at[0, block], right, kinds["on_right"](me)
+            )
+            ring_came(base + 2 + block, rel.at[1, block], kinds["far"](behind))
+            add(own.at[2, 2 + block], rel.at[1, block])
+            ring_go(
+                base + 10 + block, own.at[2, 2 + block], fin.at[1, 2 + block], left,
+                kinds["on_left"](me),
+            )
+
+    def ring_end(base, own, rel, fin, right, left, me, kinds):
+        before, behind = after(me, 3), after(me, 1)
         for block in range(2):
-            ring_came(base + block, rel.at[0, block])
-            add(own.at[1, block], rel.at[0, block])
-            ring_go(base + 8 + block, own.at[1, block], fin.at[0, block], right)
-            ring_came(base + 2 + block, rel.at[1, block])
-            add(own.at[2, 2 + block], rel.at[1, block])
-            ring_go(base + 10 + block, own.at[2, 2 + block], fin.at[1, 2 + block], left)
-
-    def ring_end(base, own, rel, fin, right, left):
-        for block in range(2):
-            ring_came(base + 4 + block, fin.at[0, 2 + block])
-            ring_came(base + 6 + block, fin.at[1, block])
-            ring_came(base + 8 + block, fin.at[0, block])
-            ring_came(base + 10 + block, fin.at[1, 2 + block])
+            ring_came(base + 4 + block, fin.at[0, 2 + block], kinds["right"](before))
+            ring_came(base + 6 + block, fin.at[1, block], kinds["left"](behind))
+            ring_came(base + 8 + block, fin.at[0, block], kinds["on_right"](before))
+            ring_came(base + 10 + block, fin.at[1, 2 + block], kinds["on_left"](behind))
 
     locals_y[0].wait()
     ring_far(*rings[1])
@@ -746,8 +818,8 @@
     f_send(3)
 
     merge(3)
+    ring_relay(*rings[0])
     ring_relay(*rings[1])
-    ring_relay(*rings[0])
     top = (z == 0) & (y == 0)
 
     @pl.when(top)
@@ -782,10 +854,15 @@
 
         lax.fori_loop(0, BLK_DEV, one, 0)
 
+    ring_end(*rings[0])
+    total(ownz, finz, ((acck, out_k, 0), (accv, out_v, 0), (accq, out_q, 1)))
     ring_end(*rings[1])
     total(owny, finy, ((accq, out_q, 0), (acck, out_k, 1), (accv, out_v, 1)))
-    ring_end(*rings[0])
-    total(ownz, finz, ((acck, out_k, 0), (accv, out_v, 0), (accq, out_q, 1)))
+
+    for condition, copy in started_if:
+        @pl.when(condition)
+        def _(copy=copy):
+            copy.wait_send()
 
     for copy in started:
         copy.wait_send()
@@ -872,14 +949,14 @@
             vmem((2, 2, BLOCK, HD), bf16),
             vmem((16, BLOCK, HD), f32),
             vmem((32, BLOCK, HD), f32),
-            vmem((2, BLOCK, HD), f32),
-            vmem((2, BLOCK, HD), bf16),
+            vmem((2, 2, BLOCK, HD), f32),
+            vmem((2, 2, BLOCK, HD), bf16),
             vmem((16, BLOCK, HD), bf16),
             vmem((32, BLOCK, HD), bf16),
             vmem((2, BLOCK, HD), bf16),
             dma,
             dma((2, 2, 4)),
-            dma,
+            dma((2,)),
             dma((2, 32)),
             dma((2, 32)),
         ],
@@ -909,8 +986,8 @@
             vmem((2, BLOCK, WIDTH), bf16),
             dma((26,)),
             dma((26,)),
-            dma((24,)),
-            dma((24,)),
+            dma((24, 2)),
+            dma((24, 2)),
             dma((12,)),
         ],
         compiler_params=pltpu.CompilerParams(

time: 198 us -> 192 us (0.970)
  Pallas kernels: 192 us -> 188 us
    pallas_call x1, Pallas kernels: 74.3 us -> 71 us  [body(): pl.pallas_call(scatter_kernel, out_shape=[shape(blocked, bf16)] * 3, in_s...]
where the time goes in v6:
time: 192 us; the launch traced here: 190 us
  Pallas kernels  188 us (98%)
    pallas_call x1, Pallas kernels, body(): pl.pallas_call(gather_kernel, out_shape=[zs] * 4 + [shape((32, 8, BLOCK),...  83.1 us
    pallas_call x1, Pallas kernels, body(): pl.pallas_call(scatter_kernel, out_shape=[shape(blocked, bf16)] * 3, in_s...  71 us
    pallas_call x1, Pallas kernels, body(): pl.pallas_call(pair_kernel, out_shape=[shape((32, 3, BLOCK, HD), bf16), s...  31.2 us

profile of v6, /device:TPU:0, one launch (start us, length us, event | category | flops | bytes accessed | tf_op | source)
XLA Modules:
  0.0 190.4 jit_solution(11553387323283032302)
XLA Ops:
  0.6 1.4 copy.10.selected
  2.0 83.1 %gather.1 = (bf16[32,512,128]{2,1,0:T(8,128)(2,1)}, bf16[32,512,128]{2,1,0:T(8,128)(2,1)}, bf16[32,512,128]{2,1,0:T(8,128)(2,1)}, bf16[32,512,128]{2,1,0:T(8,128...) custom-call(bf16[4,512,256]{2,1,0:T(8,128)(2,1)} %bitcast.7, ...), custom_call_target="tpu_custom_call" | custom-call | tf_op jit(solution)/shard_map/gather/pallas_call | solution.py:907
  85.1 31.2 %pairs.1 = (bf16[32,3,512,128]{3,2,1,0:T(8,128)(2,1)}, bf16[16,3,512,128]{3,2,1,0:T(8,128)(2,1)}) custom-call(s32[128,3]{1,0:T(8,128)} %copy.10.selected, bf16[32,512,128]{2,1,0:T(8,128)(2,1)} %get-tuple-element.25.kz, bf16[32,512,128]{2,1,0:T(8,128)(2,1)} %get-tuple-element.26.vz, bf16[32,512,128]{2,1,0:T(8,128)(2,1)} %get-tuple-element.27.qz, ...), custom_call_target="tpu_custom_call" | custom-call | tf_op jit(solution)/shard_map/pairs/pallas_call | solution.py:938
  116.4 71.0 %scatter.1 = (bf16[4,512,256]{2,1,0:T(8,128)(2,1)}, bf16[4,512,256]{2,1,0:T(8,128)(2,1)}, bf16[4,512,256]{2,1,0:T(8,128)(2,1)}) custom-call(bf16[32,3,512,128]{3,2,1,0:T(8,128)(2,1)} %get-tuple-element.35.pz, bf16[16,3,512,128]{3,2,1,0:T(8,128)(2,1)} %get-tuple-element.36.py, f32[4,512,256]{2,1,0:T(8,128)} %get-tuple-element.37.own_q, ...), custom_call_target="tpu_custom_call" | custom-call | tf_op jit(solution)/shard_map/scatter/pallas_call | solution.py:967
  187.4 2.8 %keep.1 = (bf16[4,512,256]{2,1,0:T(8,128)(2,1)}, bf16[4,512,256]{2,1,0:T(8,128)(2,1)}, bf16[4,512,256]{2,1,0:T(8,128)(2,1)}) custom-call(bf16[4,512,256]{2,1,0:T(8,128)(2,1)} %get-tuple-element.41.in_q, bf16[4,512,256]{2,1,0:T(8,128)(2,1)} %get-tuple-element.42.in_k, bf16[4,512,256]{2,1,0:T(8,128)(2,1)} %get-tuple-element.43.in_v), custom_call_target="tpu_custom_call" | custom-call | tf_op jit(solution)/shard_map/keep/pallas_call | solution.py:998

commit v7 on v6

--- a/solution.py
+++ b/solution.py
@@ -397,15 +397,14 @@
     row_at = lax.broadcasted_iota(jnp.int32, (32, 1), 0)
     group, core, block = row_at >> 3, (row_at >> 2) & 1, row_at & 3
     if head == 0:
-        slab = selected[pl.ds(pl.multiple_of(z * 32, 32), 32), :]
+        token_block = row_at + z * 32
     else:
-        slab = jnp.concatenate(
-            [selected[pl.ds(pl.multiple_of(at * 32 + y * 8, 8), 8), :] for at in range(4)], axis=0
-        )
+        token_block = group * 32 + y * 8 + (row_at & 7)
     lane = lax.broadcasted_iota(jnp.int32, (32, 128), 1)
     found = jnp.zeros((32, 128), jnp.int32)
     for pick in range(3):
-        chosen = slab[:, pick : pick + 1]
+        row = selected[pl.ds(pick, 1), :]
+        chosen = jnp.sum(jnp.where(lane == token_block, row, 0), axis=1, keepdims=True)
         z_of, y_of, c_of, b_of = chosen >> 5, (chosen >> 3) & 3, (chosen >> 2) & 1, chosen & 3
         if head == 0:
             here = (chosen > 0) & (y_of == y) & (core == c)
@@ -724,19 +723,29 @@
         (12, owny, rely, finy, near["yr"], near["yl"], y, y_kinds),
     )
 
+    def source(base, own, j, block):
+        return own.at[j, block] if base == 0 else py.at[after(y, hops[j]) * BLK_DEV + block]
+
+
     def ring_far(base, own, rel, fin, right, left, me, kinds):
         groups = kinds["far"](me)
         for block in range(2):
-            ring_go(base + block, own.at[0, block], rel.at[0, block], right, groups)
-            ring_go(base + 2 + block, own.at[0, 2 + block], rel.at[1, block], left, groups)
+            ring_go(base + block, source(base, own, 0, block), rel.at[0, block], right, groups)
+            ring_go(base + 2 + block, source(base, own, 0, 2 + block), rel.at[1, block], left, groups)
 
     def ring_right(base, own, rel, fin, right, left, me, kinds):
         for block in range(2, 4):
-            ring_go(base + 2 + block, own.at[1, block], fin.at[0, block], right, kinds["right"](me))
+            ring_go(
+                base + 2 + block, source(base, own, 1, block), fin.at[0, block], right,
+                kinds["right"](me),
+            )
 
     def ring_left(base, own, rel, fin, right, left, me, kinds):
         for block in range(2):
-            ring_go(base + 6 + block, own.at[2, block], fin.at[1, block], left, kinds["left"](me))
+            ring_go(
+                base + 6 + block, source(base, own, 2, block), fin.at[1, block], left,
+                kinds["left"](me),
+            )
 
     def ring_relay(base, own, rel, fin, right, left, me, kinds):
         before, behind = after(me, 3), after(me, 1)
@@ -761,7 +770,6 @@
             ring_came(base + 8 + block, fin.at[0, block], kinds["on_right"](before))
             ring_came(base + 10 + block, fin.at[1, 2 + block], kinds["on_left"](behind))
 
-    locals_y[0].wait()
     ring_far(*rings[1])
     merge(0)
     ring_far(*rings[0])
@@ -796,9 +804,7 @@
     f_send(0)
     f_send(1)
 
-    locals_y[1].wait()
     ring_right(*rings[1])
-    locals_y[2].wait()
     ring_left(*rings[1])
     merge(1)
     ring_right(*rings[0])
@@ -818,6 +824,8 @@
     f_send(3)
 
     merge(3)
+    for copy in locals_y:
+        copy.wait()
     ring_relay(*rings[0])
     ring_relay(*rings[1])
     top = (z == 0) & (y == 0)
@@ -827,7 +835,6 @@
         f_take(3)
         f_take(4)
 
-    locals_y[3].wait()
     for copy in locals_own:
         copy.wait()
 
@@ -962,7 +969,7 @@
         ],
         compiler_params=pltpu.CompilerParams(vmem_limit_bytes=VMEM),
         name="pairs",
-    )(selected, kz, vz, qz, gz, qy, gy, ky, vy, sz, sy)
+    )(selected.T, kz, vz, qz, gz, qy, gy, ky, vy, sz, sy)
     piece = (BLK_DEV, 3, BLOCK, HD)
     out_q, out_k, out_v = pl.pallas_call(
         scatter_kernel,

time: 192 us -> 190 us (0.990)
  no operation moved by 1% of the time
where the time goes in v7:
time: 190 us; the launch traced here: 188 us
  Pallas kernels  187 us (98%)
    pallas_call x1, Pallas kernels, body(): pl.pallas_call(gather_kernel, out_shape=[zs] * 4 + [shape((32, 8, BLOCK),...  83.2 us
    pallas_call x1, Pallas kernels, body(): pl.pallas_call(scatter_kernel, out_shape=[shape(blocked, bf16)] * 3, in_s...  69.4 us
    pallas_call x1, Pallas kernels, body(): pl.pallas_call(pair_kernel, out_shape=[shape((32, 3, BLOCK, HD), bf16), s...  31.5 us

profile of v7, /device:TPU:0, one launch (start us, length us, event | category | flops | bytes accessed | tf_op | source)
XLA Modules:
  0.0 187.7 jit_solution(5030521168359020434)
XLA Ops:
  0.6 83.2 %gather.1 = (bf16[32,512,128]{2,1,0:T(8,128)(2,1)}, bf16[32,512,128]{2,1,0:T(8,128)(2,1)}, bf16[32,512,128]{2,1,0:T(8,128)(2,1)}, bf16[32,512,128]{2,1,0:T(8,128...) custom-call(bf16[4,512,256]{2,1,0:T(8,128)(2,1)} %bitcast.8, ...), custom_call_target="tpu_custom_call" | custom-call | tf_op jit(solution)/shard_map/gather/pallas_call | solution.py:914
  83.8 31.5 %pairs.1 = (bf16[32,3,512,128]{3,2,1,0:T(8,128)(2,1)}, bf16[16,3,512,128]{3,2,1,0:T(8,128)(2,1)}) custom-call(s32[3,128]{1,0:T(4,128)} %bitcast.12, bf16[32,512,128]{2,1,0:T(8,128)(2,1)} %get-tuple-element.25.kz, bf16[32,512,128]{2,1,0:T(8,128)(2,1)} %get-tuple-element.26.vz, bf16[32,512,128]{2,1,0:T(8,128)(2,1)} %get-tuple-element.27.qz, ...), custom_call_target="tpu_custom_call" | custom-call | tf_op jit(solution)/shard_map/pairs/pallas_call | solution.py:945
  115.3 69.4 %scatter.1 = (bf16[4,512,256]{2,1,0:T(8,128)(2,1)}, bf16[4,512,256]{2,1,0:T(8,128)(2,1)}, bf16[4,512,256]{2,1,0:T(8,128)(2,1)}) custom-call(bf16[32,3,512,128]{3,2,1,0:T(8,128)(2,1)} %get-tuple-element.35.pz, bf16[16,3,512,128]{3,2,1,0:T(8,128)(2,1)} %get-tuple-element.36.py, f32[4,512,256]{2,1,0:T(8,128)} %get-tuple-element.37.own_q, ...), custom_call_target="tpu_custom_call" | custom-call | tf_op jit(solution)/shard_map/scatter/pallas_call | solution.py:974
  184.8 2.8 %keep.1 = (bf16[4,512,256]{2,1,0:T(8,128)(2,1)}, bf16[4,512,256]{2,1,0:T(8,128)(2,1)}, bf16[4,512,256]{2,1,0:T(8,128)(2,1)}) custom-call(bf16[4,512,256]{2,1,0:T(8,128)(2,1)} %get-tuple-element.41.in_q, bf16[4,512,256]{2,1,0:T(8,128)(2,1)} %get-tuple-element.42.in_k, bf16[4,512,256]{2,1,0:T(8,128)(2,1)} %get-tuple-element.43.in_v), custom_call_target="tpu_custom_call" | custom-call | tf_op jit(solution)/shard_map/keep/pallas_call | solution.py:1005
